TPU v7x, 512 devices: a whole 4x8x8 slice. The times are simulated.
512 devices in a mesh: section: 16 (over z, core), expert: 32 (over y, x).
Axes of the slice: x: 4, y: 8, z: 8, core: 2. Of those that a mesh axis runs over, the one named last changes fastest.
Arguments:
- tokens: bfloat16 [192, 4096], P('expert'), may hold values from -6 to 6
- expert_ids: int32 [16, 192, 1], P('section', 'expert'), may hold values from 0 to 3; in each aligned block of 6 rows (0 to 5, 6 to 11, ..., all dimensions but the last counted through in order) at most 2 rows name the same one
- gate_scale: float32 [16, 192], P('section', 'expert'), may hold values from 0.3 to 1
- norm_gain: float32 [16, 4096], P('section'), may hold values from 0.5 to 1.5
- w_gate: bfloat16 [16, 4096, 4096], P('section', None, 'expert'), may hold values from -0.09375 to 0.09375
- w_up: bfloat16 [16, 4096, 4096], P('section', None, 'expert'), may hold values from -0.09375 to 0.09375
- w_down: bfloat16 [16, 4096, 4096], P('section', 'expert'), may hold values from -0.1875 to 0.1875
Outputs:
- section_out: bfloat16 [16, 192, 4096], P('section', 'expert')
Inputs may be any that keep to these rules, and one draw needn't show every extreme that they name: `expert_ids`: within each layer, the 6 tokens of one index of expert choose any one expert at most 2 times.
All inputs are finite; a program needn't handle non-finite values.
Results may differ from a plain program's by a relative error of at most 0.035.
Values may be sent and summed in bfloat16 or wider, within the bound.
A program may use at most 64 MiB of HBM per device.

v0:
```python
import jax
import jax.numpy as jnp
from jax import lax
from jax.sharding import PartitionSpec as P

EXPERTS = 4
CAP = 2


def shifted(value, axis, steps):
    count = lax.axis_size(axis)
    initial, last = (max(0, -steps), min(count, count - steps))
    return lax.ppermute(value, axis, [(source, source + steps) for source in range(initial, last)])


def local(tokens, expert_ids, gate_scale, norm_gain, w_gate, w_up, w_down):
    peers = lax.axis_size("expert")
    sections = lax.axis_size("section")
    tok_rows = tokens.shape[0]
    width_model = tokens.shape[1]
    group = peers // EXPERTS
    section_index = lax.axis_index("section")
    chosen = expert_ids[0, :, 0]
    positions = jnp.arange(tok_rows)
    earlier = positions[None, :] < positions[:, None]
    same = chosen[:, None] == chosen[None, :]
    rank = jnp.sum(jnp.where(same & earlier, 1, 0), axis=1)
    match_expert = chosen[None, None, :] == jnp.arange(EXPERTS)[:, None, None]
    match_slot = rank[None, None, :] == jnp.arange(CAP)[None, :, None]
    table_float = jnp.where(match_expert & match_slot, 1.0, 0.0).astype(jnp.float32)
    table = table_float.astype(jnp.bfloat16)
    scales = gate_scale[0][:, None]
    gain = norm_gain[0]

    def layer(state, tick):
        values = state.astype(jnp.float32)
        inverse = lax.rsqrt(jnp.mean(values * values, axis=-1, keepdims=True) + 1e-06)
        normed = (values * inverse * gain).astype(jnp.bfloat16)

        def products(rows):
            gate = jnp.dot(rows, w_gate[0], preferred_element_type=jnp.float32)
            upward = jnp.dot(rows, w_up[0], preferred_element_type=jnp.float32)
            hidden = (jax.nn.silu(gate) * upward).astype(jnp.bfloat16)
            return jnp.dot(hidden, w_down[0], preferred_element_type=jnp.float32).astype(
                jnp.bfloat16
            )

        def skipped(rows):
            return jnp.zeros((rows.shape[0], width_model), jnp.bfloat16)

        slotted = jnp.einsum(
            "ect,td->ecd", table, normed, preferred_element_type=jnp.float32
        ).astype(jnp.bfloat16)
        outgoing = jnp.repeat(slotted, group, axis=0)
        arrived = lax.all_to_all(outgoing, "expert", split_axis=0, concat_axis=0, tiled=True)
        count = arrived.shape[1]
        rows = arrived.reshape(peers * count, width_model)
        partial_value = lax.cond(section_index == tick, products, skipped, rows)
        partial_value = partial_value.reshape(peers, count, width_model)
        returned = lax.all_to_all(partial_value, "expert", split_axis=0, concat_axis=0, tiled=True)
        summed = jnp.sum(
            returned.reshape(EXPERTS, group, CAP, width_model).astype(jnp.float32), axis=1
        )
        expert_out = jnp.einsum("ect,ecd->td", table_float, summed)
        return (values + scales * expert_out).astype(jnp.bfloat16)

    def tick_step(tick, carry):
        state, outputs = carry
        result = layer(state, tick)
        outputs = jnp.where(section_index == tick, result[None], outputs)
        return (shifted(result, "section", 1), outputs)

    empty = jnp.zeros((1, tok_rows, width_model), jnp.bfloat16)
    state, outputs = lax.fori_loop(0, sections - 1, tick_step, (tokens, empty))
    result = layer(state, sections - 1)
    return jnp.where(section_index == sections - 1, result[None], outputs)


def solution(mesh):
    return jax.shard_map(
        local,
        mesh=mesh,
        in_specs=(
            P("expert", None),
            P("section", "expert", None),
            P("section", "expert"),
            P("section", None),
            P("section", None, "expert"),
            P("section", None, "expert"),
            P("section", "expert", None),
        ),
        out_specs=P("section", "expert", None),
        check_vma=False,
    )
```

profile of v0, /device:TPU:64, one launch (start us, length us, event | category | flops | bytes accessed | tf_op | source)
XLA Modules:
  0.0 815.7 jit_solution(3774802553068446405)
XLA Ops:
  1.6 769.4 %while.18 = (s32[]{:T(128)}, bf16[6,4096]{1,0:T(8,128)(2,1)S(1)}, bf16[1,6,4096]{2,1,0:T(8,128)(2,1)S(1)}, f32[6,1]{0,1:T(1,128)S(1)}, s32[]{:T(128)}, /*index=5...) while((s32[]{:T(128)}, bf16[6,4096]{1,0:T(8,128)(2,1)S(1)}, ...), condition=%wide.region_6.7_spmd.clone.clone.clone, body=%wide.region_1.6_spmd.clone.clone.clone.sunk | while | flops 203268352 | bytes 20365856 | solution.py:74
  3.3 10.0 %all-to-all-start = ((bf16[32,2,4096]{2,1,0:T(2,128)(2,1)}), bf16[32,2,4096]{2,1,0:T(2,128)(2,1)S(1)}, u32[]{:S(2)}, u32[]{:S(2)}) async-start(bf16[32,2,4096]{2,1,0:T(2,128)(2,1)} %bitcast.95), calls=%async_computation | async-start | bytes 1048576 | tf_op jit(solution)/shard_map/while/body/eval_jaxpr/all_to_all | solution.py:55
  13.3 17.7 %all-to-all-done = bf16[32,2,4096]{2,1,0:T(2,128)(2,1)S(1)} async-done(((bf16[32,2,4096]{2,1,0:T(2,128)(2,1)}), bf16[32,2,4096]{2,1,0:T(2,128)(2,1)S(1)}, u32[]{:S(2)}, u32[]{:S(2)}) %all-to-all-start) | async-done | bytes 524320 | tf_op jit(solution)/shard_map/while/body/eval_jaxpr/all_to_all | solution.py:55
  32.2 4.7 all-to-all-start.1
  36.9 16.9 %all-to-all-done.1 = bf16[32,2,4096]{2,1,0:T(2,128)(2,1)S(1)} async-done(((bf16[32,2,4096]{2,1,0:T(2,128)(2,1)}), bf16[32,2,4096]{2,1,0:T(2,128)(2,1)S(1)}, u32[]{:S(2)}, u32[]{:S(2)}) %all-to-all-start.1) | async-done | bytes 524320 | tf_op jit(solution)/shard_map/while/body/eval_jaxpr/all_to_all | solution.py:60
  61.9 4.5 all-to-all-start
  66.5 18.1 %all-to-all-done = bf16[32,2,4096]{2,1,0:T(2,128)(2,1)S(1)} async-done(((bf16[32,2,4096]{2,1,0:T(2,128)(2,1)}), bf16[32,2,4096]{2,1,0:T(2,128)(2,1)S(1)}, u32[]{:S(2)}, u32[]{:S(2)}) %all-to-all-start) | async-done | bytes 524320 | tf_op jit(solution)/shard_map/while/body/eval_jaxpr/all_to_all | solution.py:55
  85.7 4.6 all-to-all-start.1
  90.3 17.1 %all-to-all-done.1 = bf16[32,2,4096]{2,1,0:T(2,128)(2,1)S(1)} async-done(((bf16[32,2,4096]{2,1,0:T(2,128)(2,1)}), bf16[32,2,4096]{2,1,0:T(2,128)(2,1)S(1)}, u32[]{:S(2)}, u32[]{:S(2)}) %all-to-all-start.1) | async-done | bytes 524320 | tf_op jit(solution)/shard_map/while/body/eval_jaxpr/all_to_all | solution.py:60
  115.5 4.5 all-to-all-start
  120.0 18.1 %all-to-all-done = bf16[32,2,4096]{2,1,0:T(2,128)(2,1)S(1)} async-done(((bf16[32,2,4096]{2,1,0:T(2,128)(2,1)}), bf16[32,2,4096]{2,1,0:T(2,128)(2,1)S(1)}, u32[]{:S(2)}, u32[]{:S(2)}) %all-to-all-start) | async-done | bytes 524320 | tf_op jit(solution)/shard_map/while/body/eval_jaxpr/all_to_all | solution.py:55
  141.7 4.6 all-to-all-start.1
  146.3 15.1 %all-to-all-done.1 = bf16[32,2,4096]{2,1,0:T(2,128)(2,1)S(1)} async-done(((bf16[32,2,4096]{2,1,0:T(2,128)(2,1)}), bf16[32,2,4096]{2,1,0:T(2,128)(2,1)S(1)}, u32[]{:S(2)}, u32[]{:S(2)}) %all-to-all-start.1) | async-done | bytes 524320 | tf_op jit(solution)/shard_map/while/body/eval_jaxpr/all_to_all | solution.py:60
  173.6 17.9 %all-to-all-done = bf16[32,2,4096]{2,1,0:T(2,128)(2,1)S(1)} async-done(((bf16[32,2,4096]{2,1,0:T(2,128)(2,1)}), bf16[32,2,4096]{2,1,0:T(2,128)(2,1)S(1)}, u32[]{:S(2)}, u32[]{:S(2)}) %all-to-all-start) | async-done | bytes 524320 | tf_op jit(solution)/shard_map/while/body/eval_jaxpr/all_to_all | solution.py:55
  192.7 5.2 all-to-all-start.1
  197.9 16.6 %all-to-all-done.1 = bf16[32,2,4096]{2,1,0:T(2,128)(2,1)S(1)} async-done(((bf16[32,2,4096]{2,1,0:T(2,128)(2,1)}), bf16[32,2,4096]{2,1,0:T(2,128)(2,1)S(1)}, u32[]{:S(2)}, u32[]{:S(2)}) %all-to-all-start.1) | async-done | bytes 524320 | tf_op jit(solution)/shard_map/while/body/eval_jaxpr/all_to_all | solution.py:60
  215.2 4.4 collective-permute-start
  222.6 6.1 all-to-all-start
  228.7 16.6 %all-to-all-done = bf16[32,2,4096]{2,1,0:T(2,128)(2,1)S(1)} async-done(((bf16[32,2,4096]{2,1,0:T(2,128)(2,1)}), bf16[32,2,4096]{2,1,0:T(2,128)(2,1)S(1)}, u32[]{:S(2)}, u32[]{:S(2)}) %all-to-all-start) | async-done | bytes 524320 | tf_op jit(solution)/shard_map/while/body/eval_jaxpr/all_to_all | solution.py:55
  246.5 4.5 all-to-all-start.1
  251.1 16.5 %all-to-all-done.1 = bf16[32,2,4096]{2,1,0:T(2,128)(2,1)S(1)} async-done(((bf16[32,2,4096]{2,1,0:T(2,128)(2,1)}), bf16[32,2,4096]{2,1,0:T(2,128)(2,1)S(1)}, u32[]{:S(2)}, u32[]{:S(2)}) %all-to-all-start.1) | async-done | bytes 524320 | tf_op jit(solution)/shard_map/while/body/eval_jaxpr/all_to_all | solution.py:60
  275.6 4.4 all-to-all-start
  280.0 18.2 %all-to-all-done = bf16[32,2,4096]{2,1,0:T(2,128)(2,1)S(1)} async-done(((bf16[32,2,4096]{2,1,0:T(2,128)(2,1)}), bf16[32,2,4096]{2,1,0:T(2,128)(2,1)S(1)}, u32[]{:S(2)}, u32[]{:S(2)}) %all-to-all-start) | async-done | bytes 524320 | tf_op jit(solution)/shard_map/while/body/eval_jaxpr/all_to_all | solution.py:55
  299.4 4.6 all-to-all-start.1
  304.0 17.1 %all-to-all-done.1 = bf16[32,2,4096]{2,1,0:T(2,128)(2,1)S(1)} async-done(((bf16[32,2,4096]{2,1,0:T(2,128)(2,1)}), bf16[32,2,4096]{2,1,0:T(2,128)(2,1)S(1)}, u32[]{:S(2)}, u32[]{:S(2)}) %all-to-all-start.1) | async-done | bytes 524320 | tf_op jit(solution)/shard_map/while/body/eval_jaxpr/all_to_all | solution.py:60
  329.3 4.5 all-to-all-start
  333.8 16.0 %all-to-all-done = bf16[32,2,4096]{2,1,0:T(2,128)(2,1)S(1)} async-done(((bf16[32,2,4096]{2,1,0:T(2,128)(2,1)}), bf16[32,2,4096]{2,1,0:T(2,128)(2,1)S(1)}, u32[]{:S(2)}, u32[]{:S(2)}) %all-to-all-start) | async-done | bytes 524320 | tf_op jit(solution)/shard_map/while/body/eval_jaxpr/all_to_all | solution.py:55
  355.4 15.3 %all-to-all-done.1 = bf16[32,2,4096]{2,1,0:T(2,128)(2,1)S(1)} async-done(((bf16[32,2,4096]{2,1,0:T(2,128)(2,1)}), bf16[32,2,4096]{2,1,0:T(2,128)(2,1)S(1)}, u32[]{:S(2)}, u32[]{:S(2)}) %all-to-all-start.1) | async-done | bytes 524320 | tf_op jit(solution)/shard_map/while/body/eval_jaxpr/all_to_all | solution.py:60
  383.1 15.8 %all-to-all-done = bf16[32,2,4096]{2,1,0:T(2,128)(2,1)S(1)} async-done(((bf16[32,2,4096]{2,1,0:T(2,128)(2,1)}), bf16[32,2,4096]{2,1,0:T(2,128)(2,1)S(1)}, u32[]{:S(2)}, u32[]{:S(2)}) %all-to-all-start) | async-done | bytes 524320 | tf_op jit(solution)/shard_map/while/body/eval_jaxpr/all_to_all | solution.py:55
  404.5 15.1 %all-to-all-done.1 = bf16[32,2,4096]{2,1,0:T(2,128)(2,1)S(1)} async-done(((bf16[32,2,4096]{2,1,0:T(2,128)(2,1)}), bf16[32,2,4096]{2,1,0:T(2,128)(2,1)S(1)}, u32[]{:S(2)}, u32[]{:S(2)}) %all-to-all-start.1) | async-done | bytes 524320 | tf_op jit(solution)/shard_map/while/body/eval_jaxpr/all_to_all | solution.py:60
  432.0 15.8 %all-to-all-done = bf16[32,2,4096]{2,1,0:T(2,128)(2,1)S(1)} async-done(((bf16[32,2,4096]{2,1,0:T(2,128)(2,1)}), bf16[32,2,4096]{2,1,0:T(2,128)(2,1)S(1)}, u32[]{:S(2)}, u32[]{:S(2)}) %all-to-all-start) | async-done | bytes 524320 | tf_op jit(solution)/shard_map/while/body/eval_jaxpr/all_to_all | solution.py:55
  453.3 15.1 %all-to-all-done.1 = bf16[32,2,4096]{2,1,0:T(2,128)(2,1)S(1)} async-done(((bf16[32,2,4096]{2,1,0:T(2,128)(2,1)}), bf16[32,2,4096]{2,1,0:T(2,128)(2,1)S(1)}, u32[]{:S(2)}, u32[]{:S(2)}) %all-to-all-start.1) | async-done | bytes 524320 | tf_op jit(solution)/shard_map/while/body/eval_jaxpr/all_to_all | solution.py:60
  480.9 16.8 %all-to-all-done = bf16[32,2,4096]{2,1,0:T(2,128)(2,1)S(1)} async-done(((bf16[32,2,4096]{2,1,0:T(2,128)(2,1)}), bf16[32,2,4096]{2,1,0:T(2,128)(2,1)S(1)}, u32[]{:S(2)}, u32[]{:S(2)}) %all-to-all-start) | async-done | bytes 524320 | tf_op jit(solution)/shard_map/while/body/eval_jaxpr/all_to_all | solution.py:55
  498.9 4.5 all-to-all-start.1
  503.4 16.7 %all-to-all-done.1 = bf16[32,2,4096]{2,1,0:T(2,128)(2,1)S(1)} async-done(((bf16[32,2,4096]{2,1,0:T(2,128)(2,1)}), bf16[32,2,4096]{2,1,0:T(2,128)(2,1)S(1)}, u32[]{:S(2)}, u32[]{:S(2)}) %all-to-all-start.1) | async-done | bytes 524320 | tf_op jit(solution)/shard_map/while/body/eval_jaxpr/all_to_all | solution.py:60
  528.2 4.5 all-to-all-start
  532.7 15.8 %all-to-all-done = bf16[32,2,4096]{2,1,0:T(2,128)(2,1)S(1)} async-done(((bf16[32,2,4096]{2,1,0:T(2,128)(2,1)}), bf16[32,2,4096]{2,1,0:T(2,128)(2,1)S(1)}, u32[]{:S(2)}, u32[]{:S(2)}) %all-to-all-start) | async-done | bytes 524320 | tf_op jit(solution)/shard_map/while/body/eval_jaxpr/all_to_all | solution.py:55
  554.0 15.1 %all-to-all-done.1 = bf16[32,2,4096]{2,1,0:T(2,128)(2,1)S(1)} async-done(((bf16[32,2,4096]{2,1,0:T(2,128)(2,1)}), bf16[32,2,4096]{2,1,0:T(2,128)(2,1)S(1)}, u32[]{:S(2)}, u32[]{:S(2)}) %all-to-all-start.1) | async-done | bytes 524320 | tf_op jit(solution)/shard_map/while/body/eval_jaxpr/all_to_all | solution.py:60
  581.6 15.8 %all-to-all-done = bf16[32,2,4096]{2,1,0:T(2,128)(2,1)S(1)} async-done(((bf16[32,2,4096]{2,1,0:T(2,128)(2,1)}), bf16[32,2,4096]{2,1,0:T(2,128)(2,1)S(1)}, u32[]{:S(2)}, u32[]{:S(2)}) %all-to-all-start) | async-done | bytes 524320 | tf_op jit(solution)/shard_map/while/body/eval_jaxpr/all_to_all | solution.py:55
  602.9 15.1 %all-to-all-done.1 = bf16[32,2,4096]{2,1,0:T(2,128)(2,1)S(1)} async-done(((bf16[32,2,4096]{2,1,0:T(2,128)(2,1)}), bf16[32,2,4096]{2,1,0:T(2,128)(2,1)S(1)}, u32[]{:S(2)}, u32[]{:S(2)}) %all-to-all-start.1) | async-done | bytes 524320 | tf_op jit(solution)/shard_map/while/body/eval_jaxpr/all_to_all | solution.py:60
  630.5 15.8 %all-to-all-done = bf16[32,2,4096]{2,1,0:T(2,128)(2,1)S(1)} async-done(((bf16[32,2,4096]{2,1,0:T(2,128)(2,1)}), bf16[32,2,4096]{2,1,0:T(2,128)(2,1)S(1)}, u32[]{:S(2)}, u32[]{:S(2)}) %all-to-all-start) | async-done | bytes 524320 | tf_op jit(solution)/shard_map/while/body/eval_jaxpr/all_to_all | solution.py:55
  651.8 15.1 %all-to-all-done.1 = bf16[32,2,4096]{2,1,0:T(2,128)(2,1)S(1)} async-done(((bf16[32,2,4096]{2,1,0:T(2,128)(2,1)}), bf16[32,2,4096]{2,1,0:T(2,128)(2,1)S(1)}, u32[]{:S(2)}, u32[]{:S(2)}) %all-to-all-start.1) | async-done | bytes 524320 | tf_op jit(solution)/shard_map/while/body/eval_jaxpr/all_to_all | solution.py:60
  679.3 15.8 %all-to-all-done = bf16[32,2,4096]{2,1,0:T(2,128)(2,1)S(1)} async-done(((bf16[32,2,4096]{2,1,0:T(2,128)(2,1)}), bf16[32,2,4096]{2,1,0:T(2,128)(2,1)S(1)}, u32[]{:S(2)}, u32[]{:S(2)}) %all-to-all-start) | async-done | bytes 524320 | tf_op jit(solution)/shard_map/while/body/eval_jaxpr/all_to_all | solution.py:55
  700.7 15.1 %all-to-all-done.1 = bf16[32,2,4096]{2,1,0:T(2,128)(2,1)S(1)} async-done(((bf16[32,2,4096]{2,1,0:T(2,128)(2,1)}), bf16[32,2,4096]{2,1,0:T(2,128)(2,1)S(1)}, u32[]{:S(2)}, u32[]{:S(2)}) %all-to-all-start.1) | async-done | bytes 524320 | tf_op jit(solution)/shard_map/while/body/eval_jaxpr/all_to_all | solution.py:60
  728.2 15.8 %all-to-all-done = bf16[32,2,4096]{2,1,0:T(2,128)(2,1)S(1)} async-done(((bf16[32,2,4096]{2,1,0:T(2,128)(2,1)}), bf16[32,2,4096]{2,1,0:T(2,128)(2,1)S(1)}, u32[]{:S(2)}, u32[]{:S(2)}) %all-to-all-start) | async-done | bytes 524320 | tf_op jit(solution)/shard_map/while/body/eval_jaxpr/all_to_all | solution.py:55
  749.5 15.1 %all-to-all-done.1 = bf16[32,2,4096]{2,1,0:T(2,128)(2,1)S(1)} async-done(((bf16[32,2,4096]{2,1,0:T(2,128)(2,1)}), bf16[32,2,4096]{2,1,0:T(2,128)(2,1)S(1)}, u32[]{:S(2)}, u32[]{:S(2)}) %all-to-all-start.1) | async-done | bytes 524320 | tf_op jit(solution)/shard_map/while/body/eval_jaxpr/all_to_all | solution.py:60
  777.1 15.8 %all-to-all-done.2 = bf16[32,2,4096]{2,1,0:T(2,128)(2,1)S(1)} async-done(((bf16[32,2,4096]{2,1,0:T(2,128)(2,1)}), bf16[32,2,4096]{2,1,0:T(2,128)(2,1)S(1)}, u32[]{:S(2)}, u32[]{:S(2)}) %all-to-all-start.2) | async-done | bytes 524320 | tf_op jit(solution)/shard_map/all_to_all | solution.py:55
  795.0 19.2 %all_to_all.36 = bf16[32,2,4096]{2,1,0:T(2,128)(2,1)S(1)} all-to-all(bf16[32,2,4096]{2,1,0:T(2,128)(2,1)S(1)} %reshape.113), channel_id=1, replica_groups=mesh['section'=16,'expert'=32] {'expert'}, dimensions={0} | all-to-all | bytes 1048576 | tf_op jit(solution)/shard_map/all_to_all | solution.py:60
  (254 shorter events, 220.9 us)
Async XLA Ops:
  1.6 29.4 %copy-start = (bf16[1,4096,128]{2,1,0:T(8,128)(2,1)S(1)}, bf16[1,4096,128]{2,1,0:T(8,128)(2,1)}, u32[]{:S(2)}) copy-start(bf16[1,4096,128]{2,1,0:T(8,128)(2,1)} %get-tuple-element.464) | copy-start | bytes 3145732 | tf_op jit(solution)/shard_map/while
  3.3 27.7 %all-to-all-start = ((bf16[32,2,4096]{2,1,0:T(2,128)(2,1)}), bf16[32,2,4096]{2,1,0:T(2,128)(2,1)S(1)}, u32[]{:S(2)}, u32[]{:S(2)}) async-start(bf16[32,2,4096]{2,1,0:T(2,128)(2,1)} %bitcast.95), calls=%async_computation | async-start | bytes 1048576 | tf_op jit(solution)/shard_map/while/body/eval_jaxpr/all_to_all | solution.py:55
  32.2 21.6 %all-to-all-start.1 = ((bf16[32,2,4096]{2,1,0:T(2,128)(2,1)}), bf16[32,2,4096]{2,1,0:T(2,128)(2,1)S(1)}, u32[]{:S(2)}, u32[]{:S(2)}) async-start(bf16[32,2,4096]{2,1,0:T(2,128)(2,1)} %reshape.131), calls=%async_computation.1 | async-start | bytes 1048576 | tf_op jit(solution)/shard_map/while/body/eval_jaxpr/all_to_all | solution.py:60
  54.6 5.6 collective-permute-start
  61.9 22.6 %all-to-all-start = ((bf16[32,2,4096]{2,1,0:T(2,128)(2,1)}), bf16[32,2,4096]{2,1,0:T(2,128)(2,1)S(1)}, u32[]{:S(2)}, u32[]{:S(2)}) async-start(bf16[32,2,4096]{2,1,0:T(2,128)(2,1)} %bitcast.95), calls=%async_computation | async-start | bytes 1048576 | tf_op jit(solution)/shard_map/while/body/eval_jaxpr/all_to_all | solution.py:55
  85.7 21.7 %all-to-all-start.1 = ((bf16[32,2,4096]{2,1,0:T(2,128)(2,1)}), bf16[32,2,4096]{2,1,0:T(2,128)(2,1)S(1)}, u32[]{:S(2)}, u32[]{:S(2)}) async-start(bf16[32,2,4096]{2,1,0:T(2,128)(2,1)} %reshape.131), calls=%async_computation.1 | async-start | bytes 1048576 | tf_op jit(solution)/shard_map/while/body/eval_jaxpr/all_to_all | solution.py:60
  108.1 5.6 collective-permute-start
  115.5 22.6 %all-to-all-start = ((bf16[32,2,4096]{2,1,0:T(2,128)(2,1)}), bf16[32,2,4096]{2,1,0:T(2,128)(2,1)S(1)}, u32[]{:S(2)}, u32[]{:S(2)}) async-start(bf16[32,2,4096]{2,1,0:T(2,128)(2,1)} %bitcast.95), calls=%async_computation | async-start | bytes 1048576 | tf_op jit(solution)/shard_map/while/body/eval_jaxpr/all_to_all | solution.py:55
  141.7 19.7 %all-to-all-start.1 = ((bf16[32,2,4096]{2,1,0:T(2,128)(2,1)}), bf16[32,2,4096]{2,1,0:T(2,128)(2,1)S(1)}, u32[]{:S(2)}, u32[]{:S(2)}) async-start(bf16[32,2,4096]{2,1,0:T(2,128)(2,1)} %reshape.131), calls=%async_computation.1 | async-start | bytes 1048576 | tf_op jit(solution)/shard_map/while/body/eval_jaxpr/all_to_all | solution.py:60
  162.1 5.6 collective-permute-start
  169.5 22.1 %all-to-all-start = ((bf16[32,2,4096]{2,1,0:T(2,128)(2,1)}), bf16[32,2,4096]{2,1,0:T(2,128)(2,1)S(1)}, u32[]{:S(2)}, u32[]{:S(2)}) async-start(bf16[32,2,4096]{2,1,0:T(2,128)(2,1)} %bitcast.95), calls=%async_computation | async-start | bytes 1048576 | tf_op jit(solution)/shard_map/while/body/eval_jaxpr/all_to_all | solution.py:55
  192.7 21.8 %all-to-all-start.1 = ((bf16[32,2,4096]{2,1,0:T(2,128)(2,1)}), bf16[32,2,4096]{2,1,0:T(2,128)(2,1)S(1)}, u32[]{:S(2)}, u32[]{:S(2)}) async-start(bf16[32,2,4096]{2,1,0:T(2,128)(2,1)} %reshape.131), calls=%async_computation.1 | async-start | bytes 1048576 | tf_op jit(solution)/shard_map/while/body/eval_jaxpr/all_to_all | solution.py:60
  215.2 5.6 collective-permute-start
  220.8 24.5 %copy-start = (bf16[1,4096,128]{2,1,0:T(8,128)(2,1)S(1)}, bf16[1,4096,128]{2,1,0:T(8,128)(2,1)}, u32[]{:S(2)}) copy-start(bf16[1,4096,128]{2,1,0:T(8,128)(2,1)} %get-tuple-element.464) | copy-start | bytes 3145732 | tf_op jit(solution)/shard_map/while
  222.6 22.8 %all-to-all-start = ((bf16[32,2,4096]{2,1,0:T(2,128)(2,1)}), bf16[32,2,4096]{2,1,0:T(2,128)(2,1)S(1)}, u32[]{:S(2)}, u32[]{:S(2)}) async-start(bf16[32,2,4096]{2,1,0:T(2,128)(2,1)} %bitcast.95), calls=%async_computation | async-start | bytes 1048576 | tf_op jit(solution)/shard_map/while/body/eval_jaxpr/all_to_all | solution.py:55
  246.5 21.0 %all-to-all-start.1 = ((bf16[32,2,4096]{2,1,0:T(2,128)(2,1)}), bf16[32,2,4096]{2,1,0:T(2,128)(2,1)S(1)}, u32[]{:S(2)}, u32[]{:S(2)}) async-start(bf16[32,2,4096]{2,1,0:T(2,128)(2,1)} %reshape.131), calls=%async_computation.1 | async-start | bytes 1048576 | tf_op jit(solution)/shard_map/while/body/eval_jaxpr/all_to_all | solution.py:60
  268.3 5.6 collective-permute-start
  275.6 22.6 %all-to-all-start = ((bf16[32,2,4096]{2,1,0:T(2,128)(2,1)}), bf16[32,2,4096]{2,1,0:T(2,128)(2,1)S(1)}, u32[]{:S(2)}, u32[]{:S(2)}) async-start(bf16[32,2,4096]{2,1,0:T(2,128)(2,1)} %bitcast.95), calls=%async_computation | async-start | bytes 1048576 | tf_op jit(solution)/shard_map/while/body/eval_jaxpr/all_to_all | solution.py:55
  299.4 21.8 %all-to-all-start.1 = ((bf16[32,2,4096]{2,1,0:T(2,128)(2,1)}), bf16[32,2,4096]{2,1,0:T(2,128)(2,1)S(1)}, u32[]{:S(2)}, u32[]{:S(2)}) async-start(bf16[32,2,4096]{2,1,0:T(2,128)(2,1)} %reshape.131), calls=%async_computation.1 | async-start | bytes 1048576 | tf_op jit(solution)/shard_map/while/body/eval_jaxpr/all_to_all | solution.py:60
  321.9 5.6 collective-permute-start
  329.3 20.5 %all-to-all-start = ((bf16[32,2,4096]{2,1,0:T(2,128)(2,1)}), bf16[32,2,4096]{2,1,0:T(2,128)(2,1)S(1)}, u32[]{:S(2)}, u32[]{:S(2)}) async-start(bf16[32,2,4096]{2,1,0:T(2,128)(2,1)} %bitcast.95), calls=%async_computation | async-start | bytes 1048576 | tf_op jit(solution)/shard_map/while/body/eval_jaxpr/all_to_all | solution.py:55
  351.0 19.7 %all-to-all-start.1 = ((bf16[32,2,4096]{2,1,0:T(2,128)(2,1)}), bf16[32,2,4096]{2,1,0:T(2,128)(2,1)S(1)}, u32[]{:S(2)}, u32[]{:S(2)}) async-start(bf16[32,2,4096]{2,1,0:T(2,128)(2,1)} %reshape.131), calls=%async_computation.1 | async-start | bytes 1048576 | tf_op jit(solution)/shard_map/while/body/eval_jaxpr/all_to_all | solution.py:60
  371.4 5.6 collective-permute-start
  378.8 20.1 %all-to-all-start = ((bf16[32,2,4096]{2,1,0:T(2,128)(2,1)}), bf16[32,2,4096]{2,1,0:T(2,128)(2,1)S(1)}, u32[]{:S(2)}, u32[]{:S(2)}) async-start(bf16[32,2,4096]{2,1,0:T(2,128)(2,1)} %bitcast.95), calls=%async_computation | async-start | bytes 1048576 | tf_op jit(solution)/shard_map/while/body/eval_jaxpr/all_to_all | solution.py:55
  400.1 19.4 %all-to-all-start.1 = ((bf16[32,2,4096]{2,1,0:T(2,128)(2,1)}), bf16[32,2,4096]{2,1,0:T(2,128)(2,1)S(1)}, u32[]{:S(2)}, u32[]{:S(2)}) async-start(bf16[32,2,4096]{2,1,0:T(2,128)(2,1)} %reshape.131), calls=%async_computation.1 | async-start | bytes 1048576 | tf_op jit(solution)/shard_map/while/body/eval_jaxpr/all_to_all | solution.py:60
  420.3 5.6 collective-permute-start
  427.6 20.1 %all-to-all-start = ((bf16[32,2,4096]{2,1,0:T(2,128)(2,1)}), bf16[32,2,4096]{2,1,0:T(2,128)(2,1)S(1)}, u32[]{:S(2)}, u32[]{:S(2)}) async-start(bf16[32,2,4096]{2,1,0:T(2,128)(2,1)} %bitcast.95), calls=%async_computation | async-start | bytes 1048576 | tf_op jit(solution)/shard_map/while/body/eval_jaxpr/all_to_all | solution.py:55
  449.0 19.4 %all-to-all-start.1 = ((bf16[32,2,4096]{2,1,0:T(2,128)(2,1)}), bf16[32,2,4096]{2,1,0:T(2,128)(2,1)S(1)}, u32[]{:S(2)}, u32[]{:S(2)}) async-start(bf16[32,2,4096]{2,1,0:T(2,128)(2,1)} %reshape.131), calls=%async_computation.1 | async-start | bytes 1048576 | tf_op jit(solution)/shard_map/while/body/eval_jaxpr/all_to_all | solution.py:60
  469.2 5.6 collective-permute-start
  476.5 21.2 %all-to-all-start = ((bf16[32,2,4096]{2,1,0:T(2,128)(2,1)}), bf16[32,2,4096]{2,1,0:T(2,128)(2,1)S(1)}, u32[]{:S(2)}, u32[]{:S(2)}) async-start(bf16[32,2,4096]{2,1,0:T(2,128)(2,1)} %bitcast.95), calls=%async_computation | async-start | bytes 1048576 | tf_op jit(solution)/shard_map/while/body/eval_jaxpr/all_to_all | solution.py:55
  498.9 21.2 %all-to-all-start.1 = ((bf16[32,2,4096]{2,1,0:T(2,128)(2,1)}), bf16[32,2,4096]{2,1,0:T(2,128)(2,1)S(1)}, u32[]{:S(2)}, u32[]{:S(2)}) async-start(bf16[32,2,4096]{2,1,0:T(2,128)(2,1)} %reshape.131), calls=%async_computation.1 | async-start | bytes 1048576 | tf_op jit(solution)/shard_map/while/body/eval_jaxpr/all_to_all | solution.py:60
  520.8 5.6 collective-permute-start
  528.2 20.3 %all-to-all-start = ((bf16[32,2,4096]{2,1,0:T(2,128)(2,1)}), bf16[32,2,4096]{2,1,0:T(2,128)(2,1)S(1)}, u32[]{:S(2)}, u32[]{:S(2)}) async-start(bf16[32,2,4096]{2,1,0:T(2,128)(2,1)} %bitcast.95), calls=%async_computation | async-start | bytes 1048576 | tf_op jit(solution)/shard_map/while/body/eval_jaxpr/all_to_all | solution.py:55
  549.7 19.4 %all-to-all-start.1 = ((bf16[32,2,4096]{2,1,0:T(2,128)(2,1)}), bf16[32,2,4096]{2,1,0:T(2,128)(2,1)S(1)}, u32[]{:S(2)}, u32[]{:S(2)}) async-start(bf16[32,2,4096]{2,1,0:T(2,128)(2,1)} %reshape.131), calls=%async_computation.1 | async-start | bytes 1048576 | tf_op jit(solution)/shard_map/while/body/eval_jaxpr/all_to_all | solution.py:60
  569.9 5.6 collective-permute-start
  577.2 20.1 %all-to-all-start = ((bf16[32,2,4096]{2,1,0:T(2,128)(2,1)}), bf16[32,2,4096]{2,1,0:T(2,128)(2,1)S(1)}, u32[]{:S(2)}, u32[]{:S(2)}) async-start(bf16[32,2,4096]{2,1,0:T(2,128)(2,1)} %bitcast.95), calls=%async_computation | async-start | bytes 1048576 | tf_op jit(solution)/shard_map/while/body/eval_jaxpr/all_to_all | solution.py:55
  598.5 19.4 %all-to-all-start.1 = ((bf16[32,2,4096]{2,1,0:T(2,128)(2,1)}), bf16[32,2,4096]{2,1,0:T(2,128)(2,1)S(1)}, u32[]{:S(2)}, u32[]{:S(2)}) async-start(bf16[32,2,4096]{2,1,0:T(2,128)(2,1)} %reshape.131), calls=%async_computation.1 | async-start | bytes 1048576 | tf_op jit(solution)/shard_map/while/body/eval_jaxpr/all_to_all | solution.py:60
  618.8 5.6 collective-permute-start
  626.1 20.1 %all-to-all-start = ((bf16[32,2,4096]{2,1,0:T(2,128)(2,1)}), bf16[32,2,4096]{2,1,0:T(2,128)(2,1)S(1)}, u32[]{:S(2)}, u32[]{:S(2)}) async-start(bf16[32,2,4096]{2,1,0:T(2,128)(2,1)} %bitcast.95), calls=%async_computation | async-start | bytes 1048576 | tf_op jit(solution)/shard_map/while/body/eval_jaxpr/all_to_all | solution.py:55
  647.4 19.4 %all-to-all-start.1 = ((bf16[32,2,4096]{2,1,0:T(2,128)(2,1)}), bf16[32,2,4096]{2,1,0:T(2,128)(2,1)S(1)}, u32[]{:S(2)}, u32[]{:S(2)}) async-start(bf16[32,2,4096]{2,1,0:T(2,128)(2,1)} %reshape.131), calls=%async_computation.1 | async-start | bytes 1048576 | tf_op jit(solution)/shard_map/while/body/eval_jaxpr/all_to_all | solution.py:60
  667.6 5.6 collective-permute-start
  675.0 20.1 %all-to-all-start = ((bf16[32,2,4096]{2,1,0:T(2,128)(2,1)}), bf16[32,2,4096]{2,1,0:T(2,128)(2,1)S(1)}, u32[]{:S(2)}, u32[]{:S(2)}) async-start(bf16[32,2,4096]{2,1,0:T(2,128)(2,1)} %bitcast.95), calls=%async_computation | async-start | bytes 1048576 | tf_op jit(solution)/shard_map/while/body/eval_jaxpr/all_to_all | solution.py:55
  696.3 19.4 %all-to-all-start.1 = ((bf16[32,2,4096]{2,1,0:T(2,128)(2,1)}), bf16[32,2,4096]{2,1,0:T(2,128)(2,1)S(1)}, u32[]{:S(2)}, u32[]{:S(2)}) async-start(bf16[32,2,4096]{2,1,0:T(2,128)(2,1)} %reshape.131), calls=%async_computation.1 | async-start | bytes 1048576 | tf_op jit(solution)/shard_map/while/body/eval_jaxpr/all_to_all | solution.py:60
  716.5 5.6 collective-permute-start
  723.8 20.1 %all-to-all-start = ((bf16[32,2,4096]{2,1,0:T(2,128)(2,1)}), bf16[32,2,4096]{2,1,0:T(2,128)(2,1)S(1)}, u32[]{:S(2)}, u32[]{:S(2)}) async-start(bf16[32,2,4096]{2,1,0:T(2,128)(2,1)} %bitcast.95), calls=%async_computation | async-start | bytes 1048576 | tf_op jit(solution)/shard_map/while/body/eval_jaxpr/all_to_all | solution.py:55
  745.2 19.4 %all-to-all-start.1 = ((bf16[32,2,4096]{2,1,0:T(2,128)(2,1)}), bf16[32,2,4096]{2,1,0:T(2,128)(2,1)S(1)}, u32[]{:S(2)}, u32[]{:S(2)}) async-start(bf16[32,2,4096]{2,1,0:T(2,128)(2,1)} %reshape.131), calls=%async_computation.1 | async-start | bytes 1048576 | tf_op jit(solution)/shard_map/while/body/eval_jaxpr/all_to_all | solution.py:60
  765.4 5.6 collective-permute-start
  772.7 20.1 %all-to-all-start.2 = ((bf16[32,2,4096]{2,1,0:T(2,128)(2,1)}), bf16[32,2,4096]{2,1,0:T(2,128)(2,1)S(1)}, u32[]{:S(2)}, u32[]{:S(2)}) async-start(bf16[32,2,4096]{2,1,0:T(2,128)(2,1)} %bitcast.11), calls=%async_computation.2 | async-start | bytes 1048576 | tf_op jit(solution)/shard_map/all_to_all | solution.py:55
  (19 other events, 322.3 us)
where the time goes:
time: 820 us; the launch traced here: 816 us
  waiting for transfers between devices  555 us (68%)
  starting transfers between devices  177 us (22%)
  local copies, waits for them, and re-layouts  42.6 us (5%)
  blocking collectives  19.2 us (2%)
  other arithmetic  11 us (1%)
  matrix products  10.3 us (1%)
    all_to_all x16, waiting for transfers between devices, layer(): lax.all_to_all(outgoing, 'expert', split_axis=0, concat_axis=0, tiled=True)  266 us
    all_to_all x15, waiting for transfers between devices, layer(): lax.all_to_all(partial_value, 'expert', split_axis=0, concat_axis=0, tile...  237 us
    all_to_all x16, starting transfers between devices, layer(): lax.all_to_all(outgoing, 'expert', split_axis=0, concat_axis=0, tiled=True)  77.7 us
    all_to_all x15, starting transfers between devices, layer(): lax.all_to_all(partial_value, 'expert', split_axis=0, concat_axis=0, tile...  67.6 us
    ppermute x15, waiting for transfers between devices, shifted(): lax.ppermute(value, axis, [(source, source + steps) for source in range(i...  52.3 us
    ppermute x15, starting transfers between devices, shifted(): lax.ppermute(value, axis, [(source, source + steps) for source in range(i...  31.3 us
    broadcast_in_dim x16, local copies, waits for them, and re-layouts, layer(): outgoing = jnp.repeat(slotted, group, axis=0)  20.2 us
    all_to_all x1, blocking collectives, layer(): lax.all_to_all(partial_value, 'expert', split_axis=0, concat_axis=0, tile...  19.2 us
  transfers between devices with their start and end apart: 46, of which 46 were waited for; matrix products, arithmetic and copies ran while one was open for 0% of the time, Pallas kernels for 0%

commit v1 on v0

v1 whole, which is shorter than its diff:
```python
import jax
import jax.numpy as jnp
from jax import lax
from jax.experimental import pallas as pl
from jax.experimental.pallas import tpu as pltpu
from jax.sharding import PartitionSpec as P

MESH = pl.DeviceIdType.MESH
EXPERTS = 4
LANES = 128
PARTS = 4
SLOTS = 16
LAG = 2
GRID_Y, GRID_X = 8, 4
PEERS = GRID_Y * GRID_X
SECTIONS = 16
TOK = 6
DX = (2, 1, 3, 0)


def kernel(
    tok_ref, ids_ref, scale_ref, gain_ref, wg_hbm, wu_hbm, wd_hbm, out_ref,
    wgu, wd, tok_stage, tok_recv, meta_send, meta_own, meta_next, meta_init, place_next, place_init,
    disp_send, disp_recv, init_send, part_send, part_recv, res_send, res_init, res_recv, out_send, out_recv,
    w_sem, meta_ss, meta_rs, tok_ss, tok_rs, disp_ss, disp_rs, part_ss, part_rs, res_ss, res_rs, out_ss, out_rs,
):
    s = lax.axis_index("section")
    p = lax.axis_index("expert")
    y, x = p // GRID_X, p % GRID_X
    last = SECTIONS - 1

    loads = [
        pltpu.make_async_copy(wg_hbm.at[0], wgu.at[:, pl.ds(0, LANES)], w_sem.at[0]),
        pltpu.make_async_copy(wu_hbm.at[0], wgu.at[:, pl.ds(LANES, LANES)], w_sem.at[1]),
        pltpu.make_async_copy(wd_hbm.at[0], wd, w_sem.at[2]),
    ]
    for load in loads:
        load.start()

    def everyone(act, skip_self):
        def row(k, _):
            dy = GRID_Y // 2 + ((k + 1) // 2) * (1 - 2 * (k % 2))
            base = ((y + dy) % GRID_Y) * GRID_X
            for dx in DX:
                q = base + (x + dx) % GRID_X
                if skip_self and dx == 0:
                    pl.when(q != p)(lambda q=q: act(q))
                else:
                    act(q)
            return 0

        lax.fori_loop(0, GRID_Y, row, 0)

    def send(src, dst, ss, rs, section, q):
        pltpu.make_async_remote_copy(
            src, dst, ss, rs, device_id=(section, q), device_id_type=MESH
        ).start()

    def drain(ref, sem):
        pltpu.make_async_copy(ref, ref, sem).wait()

    barrier = pltpu.get_barrier_semaphore()

    def greet(section):
        def one(q):
            pl.semaphore_signal(barrier, inc=1, device_id=(section, q), device_id_type=MESH)

        return one

    everyone(greet(s), True)
    pl.when(s > 0)(lambda: everyone(greet(s - 1), False))
    pl.when(s < last)(lambda: everyone(greet(s + 1), False))

    names = [ids_ref[0, t, 0] for t in range(TOK)]
    for t in range(TOK):
        rank = jnp.int32(0)
        for earlier in range(t):
            rank = rank + jnp.where(names[earlier] == names[t], 1, 0)
        slot = names[t] * SLOTS + rank + 2 * (p % 8)
        meta_send[0, pl.ds(t, 1), :] = jnp.full((1, LANES), slot.astype(jnp.float32))
        meta_send[1, pl.ds(t, 1), :] = jnp.full((1, LANES), scale_ref[0, t])
    meta_send[0, pl.ds(TOK, 2), :] = jnp.full((2, LANES), -1.0, jnp.float32)
    meta_send[1, pl.ds(TOK, 2), :] = jnp.zeros((2, LANES), jnp.float32)
    meta_own[p] = meta_send[...]

    @pl.when(s == 1)
    def _():
        for d in range(PEERS):
            tok_stage[d, pl.ds(0, TOK), :] = tok_ref[:, d * LANES:(d + 1) * LANES].astype(jnp.float32)
            tok_stage[d, pl.ds(TOK, 2), :] = jnp.zeros((2, LANES), jnp.float32)
        tok_recv[p] = tok_stage[p]

    met = PEERS - 1 + jnp.where(s > 0, PEERS, 0) + jnp.where(s < last, PEERS, 0)
    pl.semaphore_wait(barrier, met)

    @pl.when(s == 0)
    def _():
        everyone(lambda q: send(meta_send, meta_init.at[p], meta_ss, meta_rs.at[2], 1, q), False)

    @pl.when(s == 1)
    def _():
        everyone(lambda q: send(tok_stage.at[q], tok_recv.at[p], tok_ss, tok_rs, s, q), True)

    everyone(lambda q: send(meta_send, meta_own.at[p], meta_ss, meta_rs.at[0], s, q), True)

    @pl.when(s > 0)
    def _():
        everyone(lambda q: send(meta_send, meta_next.at[p], meta_ss, meta_rs.at[1], s - 1, q), False)

    def places(meta, place):
        for m in range(PARTS):
            slots = meta[8 * m:8 * m + 8, 0].reshape(64, LANES)
            along = jnp.transpose(slots)[:64, :]
            wanted = lax.broadcasted_iota(jnp.int32, (64, 64), 0).astype(jnp.float32)
            place[m] = jnp.where(along == wanted, 1.0, 0.0).astype(jnp.bfloat16)

    def emit(m, rows, place, staged, res, section):
        slotted = jnp.dot(place[m], rows, preferred_element_type=jnp.float32).astype(jnp.bfloat16)
        for e in range(EXPERTS):
            staged[m, e] = slotted[e * SLOTS:(e + 1) * SLOTS]
        everyone(
            lambda q: send(
                staged.at[m, q // 8], disp_recv.at[m, p], disp_ss, disp_rs.at[m], section, q
            ),
            False,
        )
        res[m] = rows
        send(res.at[m], res_recv.at[m], res_ss, res_rs.at[m], section, p)

    @pl.when(s == 1)
    def _():
        drain(meta_init, meta_rs.at[2])
        places(meta_init, place_init)
        drain(tok_recv.at[pl.ds(0, PEERS - 1)], tok_rs)

        def first(m, _):
            rows = tok_recv[pl.ds(8 * m, 8)].reshape(64, LANES).astype(jnp.bfloat16)
            emit(m, rows, place_init, init_send, res_init, 0)
            return 0

        lax.fori_loop(0, PARTS, first, 0)

    drain(meta_own.at[pl.ds(0, PEERS - 1)], meta_rs.at[0])

    @pl.when(s < last)
    def _():
        drain(meta_next, meta_rs.at[1])
        places(meta_next, place_next)

    for load in loads:
        load.wait()

    def work(m):
        drain(disp_recv.at[m], disp_rs.at[m])
        total = jnp.zeros((SLOTS, LANES), jnp.float32)
        acc = jnp.zeros((SLOTS, 2 * LANES), jnp.float32)
        for k in range(0, PEERS, 2):
            pair = []
            for c in (k, k + 1):
                values = disp_recv[m, c].astype(jnp.float32)
                total = total + values * values
                pair.append((values * gain_ref[0:1, c * LANES:(c + 1) * LANES]).astype(jnp.bfloat16))
            acc = acc + jnp.dot(
                jnp.concatenate(pair, axis=1), wgu[k * LANES:(k + 2) * LANES, :],
                preferred_element_type=jnp.float32,
            )
        inverse = lax.rsqrt(jnp.sum(total, axis=1, keepdims=True) * (1.0 / (PEERS * LANES)) + 1e-6)
        gate, upward = acc[:, :LANES] * inverse, acc[:, LANES:] * inverse
        hidden = (gate / (1.0 + jnp.exp(-gate)) * upward).astype(jnp.bfloat16)
        for k in range(0, PEERS, 4):
            part = jnp.dot(
                hidden, wd[:, k * LANES:(k + 4) * LANES], preferred_element_type=jnp.float32
            ).astype(jnp.bfloat16)
            for c in range(4):
                part_send[m, k + c] = part[:, c * LANES:(c + 1) * LANES]
        everyone(
            lambda q: send(part_send.at[m, q], part_recv.at[m, p], part_ss, part_rs.at[m], s, q), True
        )
        part_recv[m, p] = part_send[m, p]

    def own(m):
        drain(res_recv.at[m], res_rs.at[m])
        drain(part_recv.at[m, pl.ds(0, PEERS - 1)], part_rs.at[m])
        summed = []
        for e in range(EXPERTS):
            total = part_recv[m, 8 * e].astype(jnp.float32)
            for g in range(1, 8):
                total = total + part_recv[m, 8 * e + g].astype(jnp.float32)
            summed.append(total)
        summed = jnp.concatenate(summed, axis=0)
        high = summed.astype(jnp.bfloat16)
        low = (summed - high.astype(jnp.float32)).astype(jnp.bfloat16)
        meta = meta_own[pl.ds(8 * m, 8)]
        slots, scales = meta[:, 0].reshape(64, LANES), meta[:, 1].reshape(64, LANES)
        lane = (lax.broadcasted_iota(jnp.int32, (64, LANES), 1) % 64).astype(jnp.float32)
        chosen = jnp.where(slots == lane, 1.0, 0.0).astype(jnp.bfloat16)
        expert_out = jnp.dot(
            chosen, jnp.concatenate([high, low], axis=0), preferred_element_type=jnp.float32
        )
        rows = (res_recv[m].astype(jnp.float32) + scales * expert_out).astype(jnp.bfloat16)
        pl.when(s < last)(lambda: emit(m, rows, place_next, disp_send, res_send, s + 1))
        out_send[m] = rows.astype(jnp.float32).reshape(8, 8, LANES)
        for j in range(8):
            q = 8 * m + j

            @pl.when(q != p)
            def _():
                send(out_send.at[m, j], out_recv.at[p], out_ss, out_rs, s, q)

            @pl.when(q == p)
            def _():
                out_recv[p] = out_send[m, j]

    def step(i, _):
        pl.when(i < PARTS)(lambda: work(i))
        pl.when(i >= LAG)(lambda: own(i - LAG))
        return 0

    lax.fori_loop(0, PARTS + LAG, step, 0)

    drain(out_recv.at[pl.ds(0, PEERS - 1)], out_rs)
    for d in range(PEERS):
        out_ref[0, :, d * LANES:(d + 1) * LANES] = out_recv[d, 0:TOK, :].astype(jnp.bfloat16)

    drain(meta_own.at[pl.ds(0, PEERS - 1)], meta_ss)
    pl.when(s > 0)(lambda: drain(meta_own, meta_ss))
    pl.when(s == 0)(lambda: drain(meta_own, meta_ss))

    @pl.when(s == 1)
    def _():
        drain(tok_recv.at[pl.ds(0, PEERS - 1)], tok_ss)
        drain(disp_recv, disp_ss)
        drain(res_recv, res_ss)

    @pl.when(s < last)
    def _():
        drain(disp_recv, disp_ss)
        drain(res_recv, res_ss)

    drain(part_recv.at[:, pl.ds(0, PEERS - 1)], part_ss)
    drain(out_recv.at[pl.ds(0, PEERS - 1)], out_ss)


def local(tokens, expert_ids, gate_scale, norm_gain, w_gate, w_up, w_down):
    width = tokens.shape[1]
    vmem = pl.BlockSpec(memory_space=pltpu.VMEM)
    smem = pl.BlockSpec(memory_space=pltpu.SMEM)
    hbm = pl.BlockSpec(memory_space=pl.ANY)
    b16, f32 = jnp.bfloat16, jnp.float32
    dma = pltpu.SemaphoreType.DMA
    return pl.pallas_call(
        kernel,
        out_shape=jax.ShapeDtypeStruct((1, TOK, width), b16),
        in_specs=[vmem, smem, smem, vmem, hbm, hbm, hbm],
        out_specs=vmem,
        scratch_shapes=[
            pltpu.VMEM((width, 2 * LANES), b16),
            pltpu.VMEM((LANES, width), b16),
            pltpu.VMEM((PEERS, 8, LANES), f32),
            pltpu.VMEM((PEERS, 8, LANES), f32),
            pltpu.VMEM((2, 8, LANES), f32),
            pltpu.VMEM((PEERS, 2, 8, LANES), f32),
            pltpu.VMEM((PEERS, 2, 8, LANES), f32),
            pltpu.VMEM((PEERS, 2, 8, LANES), f32),
            pltpu.VMEM((PARTS, 64, 64), b16),
            pltpu.VMEM((PARTS, 64, 64), b16),
            pltpu.VMEM((PARTS, EXPERTS, SLOTS, LANES), b16),
            pltpu.VMEM((PARTS, PEERS, SLOTS, LANES), b16),
            pltpu.VMEM((PARTS, EXPERTS, SLOTS, LANES), b16),
            pltpu.VMEM((PARTS, PEERS, SLOTS, LANES), b16),
            pltpu.VMEM((PARTS, PEERS, SLOTS, LANES), b16),
            pltpu.VMEM((PARTS, 64, LANES), b16),
            pltpu.VMEM((PARTS, 64, LANES), b16),
            pltpu.VMEM((PARTS, 64, LANES), b16),
            pltpu.VMEM((PARTS, 8, 8, LANES), f32),
            pltpu.VMEM((PEERS, 8, LANES), f32),
            dma((3,)),
            dma,
            dma((3,)),
            dma,
            dma,
            dma,
            dma((PARTS,)),
            dma,
            dma((PARTS,)),
            dma,
            dma((PARTS,)),
            dma,
            dma,
        ],
        compiler_params=pltpu.CompilerParams(
            collective_id=0, has_side_effects=True, vmem_limit_bytes=32 * 2**20
        ),
    )(tokens, expert_ids, gate_scale, norm_gain, w_gate, w_up, w_down)


def solution(mesh):
    return jax.shard_map(
        local,
        mesh=mesh,
        in_specs=(
            P("expert", None),
            P("section", "expert", None),
            P("section", "expert"),
            P("section", None),
            P("section", None, "expert"),
            P("section", None, "expert"),
            P("section", "expert", None),
        ),
        out_specs=P("section", "expert", None),
        check_vma=False,
    )
```

time: 820 us -> 255 us (0.31)
  the two profiles are of different devices: /device:TPU:64 before, /device:TPU:505 now
where the time goes in v1:
time: 255 us
  Pallas kernels  248 us (97%)
  local copies, waits for them, and re-layouts  6.62 us (3%)
    pallas_call x1, Pallas kernels, local(): pl.pallas_call(kernel, out_shape=jax.ShapeDtypeStruct((1, TOK, width), b1...  248 us
    unnamed x14, local copies, waits for them, and re-layouts  6.62 us

profile of v1, /device:TPU:505, one launch (start us, length us, event | category | flops | bytes accessed | tf_op | source)
XLA Modules:
  0.0 254.6 jit_solution(6442875846532643715)
XLA Ops:
  0.0 0.0 copy-start.5
  0.0 0.8 copy.8.ids_ref
  0.8 0.0 copy-done.5
  0.8 0.0 copy-start
  0.8 1.2 copy-done
  2.0 0.0 copy-start.1
  2.0 1.2 copy-done.1
  3.2 0.0 copy-start.2
  3.2 1.2 copy-done.2
  4.4 0.0 copy-start.3
  4.4 0.8 copy-done.3
  5.3 0.0 copy-start.4
  5.3 0.7 copy-done.4
  6.0 248.0 %shard_map.73 = bf16[1,6,4096]{2,1,0:T(8,128)(2,1)S(1)} custom-call(bf16[6,4096]{1,0:T(8,128)(2,1)S(1)} %copy-done.3, s32[1,6,1]{2,1,0:T(8,128)S(1)} %copy.8.ids_ref, f32[1,6]{1,0:T(1,128)S(1)} %copy-done.5, f32[1,4096]{1,0:T(1,128)S(1)} %copy-done.4, bf16[1,4096,128]{2,1,0:T(8,128)(2,1)S(1)} %copy-done, bf16[1,4096,128]{2,1,0:T(8,128)(2,1)S(1)} %copy-done.1, ...), custom_call_target="tpu_custom_call" | custom-call | tf_op jit(solution)/shard_map/pallas_call | solution.py:251
  254.0 0.6 copy.10
Async XLA Ops:
  0.0 0.8 copy-start.5
  0.8 1.2 copy-start
  2.0 1.2 copy-start.1
  3.2 1.2 copy-start.2
  4.4 0.8 copy-start.3
  5.3 0.7 copy-start.4

commit v2 on v1

v2 whole, which is shorter than its diff:
```python
import jax
import jax.numpy as jnp
from jax import lax
from jax.experimental import pallas as pl
from jax.experimental.pallas import tpu as pltpu
from jax.sharding import PartitionSpec as P

MESH = pl.DeviceIdType.MESH
EXPERTS = 4
LANES = 128
PARTS = 4
SLOTS = 16
LAG = 2
GRID_Y, GRID_X = 8, 4
PEERS = GRID_Y * GRID_X
SECTIONS = 16
TOK = 6
PAIR = 2
EARLY = 2
DX = (2, 1, 3, 0)
FAR_FIRST = (4, 3, 5, 2, 6, 1, 7, 0)
NEAR_FIRST = (0, 1, 7, 2, 6, 3, 5, 4)


def kernel(
    tok_hbm, ids_ref, scale_ref, gain_hbm, wg_hbm, wu_hbm, wd_hbm, out_ref,
    wgu, wd, tok_ref, gain_ref, tok_stage, tok_recv, meta_send, meta_own, meta_next, meta_init, place_next, place_init, chosen, scales,
    disp_send, disp_recv, init_send, part_send, part_recv, res_send, res_init, res_recv, out_send, out_recv, gains, row_sums,
    pair_sums, pair_send, pair_res, pair_out,
    w_sem, move_ss, move_rs, meta_ss, meta_rs, tok_ss, tok_rs, disp_ss, disp_rs, part_ss, part_rs, res_ss, res_rs, out_ss, out_rs,
):
    s = lax.axis_index("section")
    p = lax.axis_index("expert")
    y, x = p // GRID_X, p % GRID_X
    last = SECTIONS - 1

    loads = [
        pltpu.make_async_copy(wg_hbm.at[0], wgu.at[:, pl.ds(0, LANES)], w_sem.at[0]),
        pltpu.make_async_copy(wu_hbm.at[0], wgu.at[:, pl.ds(LANES, LANES)], w_sem.at[1]),
        pltpu.make_async_copy(wd_hbm.at[0], wd.at[pl.ds(0, LANES)], w_sem.at[2]),
    ]
    near = [
        pltpu.make_async_copy(tok_hbm, tok_ref, w_sem.at[3]),
        pltpu.make_async_copy(gain_hbm, gain_ref, w_sem.at[4]),
    ]
    for load in near + loads:
        load.start()

    def row_at(r):
        return (y + r) % GRID_Y

    def in_row(r, act, skip_self):
        base = row_at(r) * GRID_X
        for dx in DX:
            if not (skip_self and r == 0 and dx == 0):
                act(base + (x + dx) % GRID_X, (GRID_Y - r) % GRID_Y)

    def everyone(act, skip_self):
        def one(k, _):
            r = GRID_Y // 2 + ((k + 1) // 2) * (1 - 2 * (k % 2))
            base = ((y + r) % GRID_Y) * GRID_X
            back = (GRID_Y - r) % GRID_Y
            for dx in DX:
                q = base + (x + dx) % GRID_X
                if skip_self and dx == 0:
                    pl.when(q != p)(lambda q=q: act(q, back))
                else:
                    act(q, back)
            return 0

        lax.fori_loop(0, GRID_Y, one, 0)

    def loop(count, body):
        lax.fori_loop(0, count, lambda k, c: (body(k), c)[1], 0)

    def send(src, dst, ss, rs, section, q):
        pltpu.make_async_remote_copy(
            src, dst, ss, rs, device_id=(section, q), device_id_type=MESH
        ).start()

    def drain(ref, sem):
        pltpu.make_async_copy(ref, ref, sem).wait()

    barrier = pltpu.get_barrier_semaphore()

    def greet(section):
        def one(q, r):
            pl.semaphore_signal(barrier, inc=1, device_id=(section, q), device_id_type=MESH)

        return one

    everyone(greet(s), True)
    pl.when(s > 0)(lambda: everyone(greet(s - 1), False))
    pl.when(s < last)(lambda: everyone(greet(s + 1), False))

    names = [ids_ref[0, t] for t in range(TOK)]
    for t in range(TOK):
        rank = jnp.int32(0)
        for earlier in range(t):
            rank = rank + jnp.where(names[earlier] == names[t], 1, 0)
        slot = names[t] * SLOTS + rank + 2 * (p % 8)
        lane = lax.broadcasted_iota(jnp.int32, (1, LANES), 1)
        meta_send[pl.ds(t, 1), :] = jnp.where(lane < 64, slot.astype(jnp.float32), scale_ref[0, t])
    lane = lax.broadcasted_iota(jnp.int32, (2, LANES), 1)
    meta_send[pl.ds(TOK, 2), :] = jnp.where(lane < 64, -1.0, 0.0)
    meta_own[p] = meta_send[...]

    for load in near:
        load.wait()

    @pl.when(s == 1)
    def _():
        def stage(d):
            columns = pl.ds(pl.multiple_of(d * LANES, LANES), LANES)
            tok_stage[d, pl.ds(0, TOK), :] = tok_ref[:, columns].astype(jnp.float32)
            tok_stage[d, pl.ds(TOK, 2), :] = jnp.zeros((2, LANES), jnp.float32)

        loop(PEERS, stage)
        tok_recv[p] = tok_stage[p]

    met = PEERS - 1 + jnp.where(s > 0, PEERS, 0) + jnp.where(s < last, PEERS, 0)
    pl.semaphore_wait(barrier, met)

    @pl.when(s == 0)
    def _():
        everyone(lambda q, r: send(meta_send, meta_init.at[p], meta_ss, meta_rs.at[2], 1, q), False)

    @pl.when(s == 1)
    def _():
        everyone(lambda q, r: send(tok_stage.at[q], tok_recv.at[p], tok_ss, tok_rs, s, q), True)

    late = s >= EARLY
    worker = (x % 2 == 0)

    def moves(q):
        return [
            pltpu.make_async_remote_copy(
                src, dst, move_ss.at[i], move_rs.at[i], device_id=(s, q), device_id_type=MESH
            )
            for i, (src, dst) in enumerate((
                (wg_hbm.at[0], wgu.at[:, pl.ds(2 * LANES, LANES)]),
                (wu_hbm.at[0], wgu.at[:, pl.ds(3 * LANES, LANES)]),
                (wd_hbm.at[0], wd.at[pl.ds(LANES, LANES)]),
            ))
        ]

    @pl.when(late & jnp.logical_not(worker))
    def _():
        aim = jnp.where(s % 2 == 0, x - 1, (x + 1) % GRID_X)
        for move in moves(y * GRID_X + aim):
            move.start()

    def places(meta, place):
        for m in range(PARTS):
            along = jnp.transpose(meta[8 * m:8 * m + 8].reshape(64, LANES))[:64, :]
            wanted = lax.broadcasted_iota(jnp.int32, (64, 64), 0).astype(jnp.float32)
            place[m] = jnp.where(along == wanted, 1.0, 0.0).astype(jnp.bfloat16)

    def emit(m, rows, place, staged, res, section):
        slotted = jnp.dot(place[m], rows, preferred_element_type=jnp.float32).astype(jnp.bfloat16)
        for e in range(EXPERTS):
            staged[m, e] = slotted[e * SLOTS:(e + 1) * SLOTS]
        everyone(
            lambda q, r: pl.when((section < EARLY) | (q % 2 == 0))(
                lambda: send(
                    staged.at[m, q // 8], disp_recv.at[m, p], disp_ss, disp_rs.at[m, r], section, q
                )
            ),
            False,
        )
        res[m] = rows
        early = section < EARLY
        keeper = jnp.where(early, p, y * GRID_X + 2 * (x // 2) + 1)
        send(
            res.at[m], res_recv.at[m, jnp.where(early, 0, x % 2)], res_ss, res_rs.at[m], section, keeper
        )

    @pl.when(s == 1)
    def _():
        drain(meta_init, meta_rs.at[2])
        places(meta_init, place_init)
        drain(tok_recv.at[pl.ds(0, PEERS - 1)], tok_rs)

        def first(m, _):
            rows = tok_recv[pl.ds(8 * m, 8)].reshape(64, LANES).astype(jnp.bfloat16)
            emit(m, rows, place_init, init_send, res_init, 0)
            return 0

        lax.fori_loop(0, PARTS, first, 0)

    everyone(lambda q, r: send(meta_send, meta_own.at[p], meta_ss, meta_rs.at[0], s, q), True)

    @pl.when(s > 0)
    def _():
        everyone(lambda q, r: send(meta_send, meta_next.at[p], meta_ss, meta_rs.at[1], s - 1, q), False)

    drain(meta_own.at[pl.ds(0, PEERS - 1)], meta_rs.at[0])
    for m in range(PARTS):
        rows = meta_own[8 * m:8 * m + 8].reshape(64, LANES)
        lane = (lax.broadcasted_iota(jnp.int32, (64, LANES), 1) % 64).astype(jnp.float32)
        chosen[m] = jnp.where(jnp.broadcast_to(rows[:, 0:1], (64, LANES)) == lane, 1.0, 0.0).astype(jnp.bfloat16)
        scales[m] = jnp.broadcast_to(rows[:, 64:65], (64, LANES))

    @pl.when(s < last)
    def _():
        drain(meta_next, meta_rs.at[1])
        places(meta_next, place_next)

    def spread(d):
        columns = pl.ds(pl.multiple_of(d * LANES, LANES), LANES)
        gains[d] = jnp.broadcast_to(gain_ref[0:1, columns], (SLOTS, LANES))

    loop(PEERS, spread)
    for load in loads:
        load.wait()

    def row_columns(row):
        return pl.ds(pl.multiple_of(row * GRID_X * LANES, GRID_X * LANES), GRID_X * LANES)

    def work(m, blocks):
        total = jnp.zeros((SLOTS, LANES), jnp.float32)
        acc = jnp.zeros((SLOTS, 2 * blocks * LANES), jnp.float32)
        for r in NEAR_FIRST:
            row = row_at(r)
            four = pl.ds(row * GRID_X, GRID_X)
            drain(disp_recv.at[m, four], disp_rs.at[m, r])
            values = disp_recv[m, four].astype(jnp.float32)
            gained = (values * gains[four]).astype(jnp.bfloat16)
            for c in range(GRID_X):
                total = total + values[c] * values[c]
            acc = acc + jnp.dot(
                jnp.concatenate([gained[c] for c in range(GRID_X)], axis=1),
                wgu[row_columns(row), pl.ds(0, 2 * blocks * LANES)],
                preferred_element_type=jnp.float32,
            )
        inverse = lax.rsqrt(jnp.sum(total, axis=1, keepdims=True) * (1.0 / (PEERS * LANES)) + 1e-6)
        hidden = []
        for b in range(blocks):
            gate = acc[:, 2 * b * LANES:(2 * b + 1) * LANES] * inverse
            upward = acc[:, (2 * b + 1) * LANES:(2 * b + 2) * LANES] * inverse
            hidden.append((gate / (1.0 + jnp.exp(-gate)) * upward).astype(jnp.bfloat16))
        hidden = jnp.concatenate(hidden, axis=1)
        for r in FAR_FIRST:
            row = row_at(r)
            part = jnp.dot(
                hidden, wd[pl.ds(0, blocks * LANES), row_columns(row)], preferred_element_type=jnp.float32
            ).astype(jnp.bfloat16)
            for c in range(GRID_X):
                part_send[m, row * GRID_X + c] = part[:, c * LANES:(c + 1) * LANES]
            back = (GRID_Y - r) % GRID_Y
            if blocks == 1:
                in_row(
                    r,
                    lambda q, r: send(
                        part_send.at[m, q], part_recv.at[m, p], part_ss, part_rs.at[m, r], s, q
                    ),
                    True,
                )
            else:
                for j in range(2):
                    send(
                        part_send.at[m, pl.ds(row * GRID_X + 2 * j, PAIR)], part_recv.at[m, pl.ds(p, PAIR)],
                        part_ss, part_rs.at[m, back], s, row * GRID_X + 2 * j + 1,
                    )
        if blocks == 1:
            part_recv[m, p] = part_send[m, p]

    def keep(m):
        for r in NEAR_FIRST:
            row = row_at(r)
            four = pl.ds(row * GRID_X, GRID_X)
            drain(part_recv.at[m, four], part_rs.at[m, r])
            values = part_recv[m, four].astype(jnp.float32)
            pair_sums[row] = values[0:2] + values[2:4]
        summed = []
        for h in range(PAIR):
            summed.append(
                jnp.concatenate([pair_sums[2 * e, h] + pair_sums[2 * e + 1, h] for e in range(EXPERTS)], axis=0)
            )
        summed = jnp.concatenate(summed, axis=1)
        high = summed.astype(jnp.bfloat16)
        low = (summed - high.astype(jnp.float32)).astype(jnp.bfloat16)
        expert_out = jnp.dot(
            chosen[m], jnp.concatenate([high, low], axis=0), preferred_element_type=jnp.float32
        )
        drain(res_recv.at[m], res_rs.at[m])
        before = jnp.concatenate([res_recv[m, h] for h in range(PAIR)], axis=1).astype(jnp.float32)
        scale = jnp.concatenate([scales[m]] * PAIR, axis=1)
        rows = (before + scale * expert_out).astype(jnp.bfloat16)

        @pl.when(s < last)
        def _():
            slotted = jnp.dot(place_next[m], rows, preferred_element_type=jnp.float32).astype(jnp.bfloat16)
            for e in range(EXPERTS):
                for h in range(PAIR):
                    pair_send[m, e, h] = slotted[e * SLOTS:(e + 1) * SLOTS, h * LANES:(h + 1) * LANES]
            for r in FAR_FIRST:
                row = row_at(r)
                for j in range(2):
                    send(
                        pair_send.at[m, row // 2], disp_recv.at[m, pl.ds(p - 1, PAIR)],
                        disp_ss, disp_rs.at[m, (GRID_Y - r) % GRID_Y], s + 1, row * GRID_X + 2 * j,
                    )
            for h in range(PAIR):
                pair_res[m, h] = rows[:, h * LANES:(h + 1) * LANES]
            send(pair_res.at[m], res_recv.at[m], res_ss, res_rs.at[m], s + 1, p)

        shown = rows.astype(jnp.float32)
        for h in range(PAIR):
            pair_out[m, :, h] = shown[:, h * LANES:(h + 1) * LANES].reshape(8, 8, LANES)
        pl.when(s == last)(lambda: deliver_pair(m))

    def deliver_pair(m):
        mine = pl.ds(p - 1, PAIR)

        def one(j):
            q = 8 * m + j
            pl.when(q != p)(lambda: send(pair_out.at[m, j], out_recv.at[mine], out_ss, out_rs, s, q))

            @pl.when(q == p)
            def _():
                out_recv[mine] = pair_out[m, j]

        loop(8, one)

    def deliver(m):
        for j in range(8):
            q = 8 * m + j

            @pl.when(q != p)
            def _():
                send(out_send.at[m, j], out_recv.at[p], out_ss, out_rs, s, q)

            @pl.when(q == p)
            def _():
                out_recv[p] = out_send[m, j]

    def own(m):
        drain(res_recv.at[m, 0], res_rs.at[m])
        for r in NEAR_FIRST:
            row = row_at(r)
            count = GRID_X - 1 if r == 0 else GRID_X
            drain(part_recv.at[m, pl.ds(row * GRID_X, count)], part_rs.at[m, r])
            four = part_recv[m, pl.ds(row * GRID_X, GRID_X)].astype(jnp.float32)
            row_sums[row] = (four[0] + four[1]) + (four[2] + four[3])
        summed = [row_sums[2 * e] + row_sums[2 * e + 1] for e in range(EXPERTS)]
        summed = jnp.concatenate(summed, axis=0)
        high = summed.astype(jnp.bfloat16)
        low = (summed - high.astype(jnp.float32)).astype(jnp.bfloat16)
        expert_out = jnp.dot(
            chosen[m], jnp.concatenate([high, low], axis=0), preferred_element_type=jnp.float32
        )
        rows = (res_recv[m, 0].astype(jnp.float32) + scales[m] * expert_out).astype(jnp.bfloat16)
        pl.when(s < last)(lambda: emit(m, rows, place_next, disp_send, res_send, s + 1))
        out_send[m] = rows.astype(jnp.float32).reshape(8, 8, LANES)
    @pl.when(s < EARLY)
    def _():
        def step(i):
            pl.when(i < PARTS)(lambda: work(i, 1))
            pl.when(i >= LAG)(lambda: own(i - LAG))

        loop(PARTS + LAG, step)
        loop(PARTS, deliver)

    @pl.when(late & worker)
    def _():
        for move in moves(p):
            move.wait_recv()
        loop(PARTS, lambda m: work(m, 2))

    @pl.when(late & jnp.logical_not(worker))
    def _():
        loop(PARTS, keep)

        @pl.when(s < last)
        def _():
            loop(PARTS, deliver_pair)

        for move in moves(p):
            move.wait_send()

    pl.when(s < EARLY)(lambda: drain(out_recv.at[pl.ds(0, PEERS - 1)], out_rs))
    pl.when(late & worker)(lambda: drain(out_recv, out_rs))
    pl.when(late & jnp.logical_not(worker))(lambda: drain(out_recv.at[pl.ds(0, PEERS - PAIR)], out_rs))

    def store(d):
        columns = pl.ds(pl.multiple_of(d * LANES, LANES), LANES)
        out_ref[0, :, columns] = out_recv[d, 0:TOK, :].astype(jnp.bfloat16)

    loop(PEERS, store)

    drain(meta_own.at[pl.ds(0, PEERS - 1)], meta_ss)
    pl.when(s > 0)(lambda: drain(meta_own, meta_ss))
    pl.when(s == 0)(lambda: drain(meta_own, meta_ss))

    half = PEERS // 2

    @pl.when(s == 0)
    def _():
        drain(disp_recv, disp_ss)
        drain(res_recv.at[:, 0], res_ss)

    @pl.when(s == 1)
    def _():
        drain(tok_recv.at[pl.ds(0, PEERS - 1)], tok_ss)
        drain(disp_recv, disp_ss)
        drain(disp_recv.at[:, pl.ds(0, half)], disp_ss)
        drain(res_recv, res_ss)

    @pl.when(s < EARLY)
    def _():
        drain(part_recv.at[:, pl.ds(0, PEERS - 1)], part_ss)
        drain(out_recv.at[pl.ds(0, PEERS - 1)], out_ss)

    pl.when(late & worker)(lambda: drain(part_recv, part_ss))

    @pl.when(late & jnp.logical_not(worker))
    def _():
        drain(out_recv, out_ss)
        drain(out_recv.at[pl.ds(0, PEERS - PAIR)], out_ss)

        @pl.when(s < last)
        def _():
            drain(disp_recv, disp_ss)
            drain(res_recv, res_ss)


def local(tokens, expert_ids, gate_scale, norm_gain, w_gate, w_up, w_down):
    width = tokens.shape[1]
    vmem = pl.BlockSpec(memory_space=pltpu.VMEM)
    smem = pl.BlockSpec(memory_space=pltpu.SMEM)
    hbm = pl.BlockSpec(memory_space=pltpu.HBM)
    b16, f32 = jnp.bfloat16, jnp.float32
    dma = pltpu.SemaphoreType.DMA
    return pl.pallas_call(
        kernel,
        out_shape=jax.ShapeDtypeStruct((1, TOK, width), b16),
        in_specs=[hbm, smem, smem, hbm, hbm, hbm, hbm],
        out_specs=vmem,
        scratch_shapes=[
            pltpu.VMEM((width, 4 * LANES), b16),
            pltpu.VMEM((2 * LANES, width), b16),
            pltpu.VMEM((TOK, width), b16),
            pltpu.VMEM((1, width), f32),
            pltpu.VMEM((PEERS, 8, LANES), f32),
            pltpu.VMEM((PEERS, 8, LANES), f32),
            pltpu.VMEM((8, LANES), f32),
            pltpu.VMEM((PEERS, 8, LANES), f32),
            pltpu.VMEM((PEERS, 8, LANES), f32),
            pltpu.VMEM((PEERS, 8, LANES), f32),
            pltpu.VMEM((PARTS, 64, 64), b16),
            pltpu.VMEM((PARTS, 64, 64), b16),
            pltpu.VMEM((PARTS, 64, LANES), b16),
            pltpu.VMEM((PARTS, 64, LANES), f32),
            pltpu.VMEM((PARTS, EXPERTS, SLOTS, LANES), b16),
            pltpu.VMEM((PARTS, PEERS, SLOTS, LANES), b16),
            pltpu.VMEM((PARTS, EXPERTS, SLOTS, LANES), b16),
            pltpu.VMEM((PARTS, PEERS, SLOTS, LANES), b16),
            pltpu.VMEM((PARTS, PEERS, SLOTS, LANES), b16),
            pltpu.VMEM((PARTS, 64, LANES), b16),
            pltpu.VMEM((PARTS, 64, LANES), b16),
            pltpu.VMEM((PARTS, PAIR, 64, LANES), b16),
            pltpu.VMEM((PARTS, 8, 8, LANES), f32),
            pltpu.VMEM((PEERS, 8, LANES), f32),
            pltpu.VMEM((PEERS, SLOTS, LANES), f32),
            pltpu.VMEM((GRID_Y, SLOTS, LANES), f32),
            pltpu.VMEM((GRID_Y, PAIR, SLOTS, LANES), f32),
            pltpu.VMEM((PARTS, EXPERTS, PAIR, SLOTS, LANES), b16),
            pltpu.VMEM((PARTS, PAIR, 64, LANES), b16),
            pltpu.VMEM((PARTS, 8, PAIR, 8, LANES), f32),
            dma((5,)),
            dma((3,)),
            dma((3,)),
            dma,
            dma((3,)),
            dma,
            dma,
            dma,
            dma((PARTS, GRID_Y)),
            dma,
            dma((PARTS, GRID_Y)),
            dma,
            dma((PARTS,)),
            dma,
            dma,
        ],
        compiler_params=pltpu.CompilerParams(
            collective_id=0, has_side_effects=True, vmem_limit_bytes=60 * 2**20
        ),
    )(tokens, expert_ids[:, :, 0], gate_scale, norm_gain, w_gate, w_up, w_down)


def solution(mesh):
    return jax.shard_map(
        local,
        mesh=mesh,
        in_specs=(
            P("expert", None),
            P("section", "expert", None),
            P("section", "expert"),
            P("section", None),
            P("section", None, "expert"),
            P("section", None, "expert"),
            P("section", "expert", None),
        ),
        out_specs=P("section", "expert", None),
        check_vma=False,
    )
```

time: 255 us -> 229 us (0.90)
  Pallas kernels: 248 us -> 227 us
  local copies, waits for them, and re-layouts: 6.62 us -> 1.47 us
    pallas_call x1, Pallas kernels: 248 us -> 227 us  [local(): pl.pallas_call(kernel, out_shape=jax.ShapeDtypeStruct((1, TOK, width), b1...]
    unnamed x14 -> x1, local copies, waits for them, and re-layouts: 6.62 us -> 1.47 us
where the time goes in v2:
time: 229 us; the launch traced here: 228 us
  Pallas kernels  227 us (99%)
    pallas_call x1, Pallas kernels, local(): pl.pallas_call(kernel, out_shape=jax.ShapeDtypeStruct((1, TOK, width), b1...  227 us

profile of v2, /device:TPU:505, one launch (start us, length us, event | category | flops | bytes accessed | tf_op | source)
XLA Modules:
  0.0 228.3 jit_solution(16105048367930148542)
XLA Ops:
  0.0 226.9 %shard_map.73 = bf16[1,6,4096]{2,1,0:T(8,128)(2,1)} custom-call(bf16[6,4096]{1,0:T(8,128)(2,1)} %tok_hbm.1, s32[1,6]{1,0:T(1,128)} %bitcast.1, f32[1,6]{1,0:T(1,128)} %scale_ref.1, f32[1,4096]{1,0:T(1,128)} %gain_hbm.1, bf16[1,4096,128]{2,1,0:T(8,128)(2,1)} %wg_hbm.1, bf16[1,4096,128]{2,1,0:T(8,128)(2,1)} %wu_hbm.1, bf16[1,128,4096]{2,1,0:T(8,128)(2,1)} %wd_hbm.1), custom_call_target="tpu_custom_call" | custom-call | tf_op jit(solution)/shard_map/pallas_call | solution.py:435
  226.9 1.5 copy.9

commit v3 on v2

--- a/solution.py
+++ b/solution.py
@@ -19,6 +19,8 @@
 EARLY = 2
 DX = (2, 1, 3, 0)
 FAR_FIRST = (4, 3, 5, 2, 6, 1, 7, 0)
+ARRIVALS = ((0, 1, 7), (2, 6), (3, 5), (4,))
+LEAVING = ((4,), (3, 5, 2, 6), (1, 7, 0))
 NEAR_FIRST = (0, 1, 7, 2, 6, 3, 5, 4)
 
 
@@ -26,7 +28,7 @@
     tok_hbm, ids_ref, scale_ref, gain_hbm, wg_hbm, wu_hbm, wd_hbm, out_ref,
     wgu, wd, tok_ref, gain_ref, tok_stage, tok_recv, meta_send, meta_own, meta_next, meta_init, place_next, place_init, chosen, scales,
     disp_send, disp_recv, init_send, part_send, part_recv, res_send, res_init, res_recv, out_send, out_recv, gains, row_sums,
-    pair_sums, pair_send, pair_res, pair_out,
+    pair_sums, pair_send, pair_res, pair_out, hop, hop_scale, placed,
     w_sem, move_ss, move_rs, meta_ss, meta_rs, tok_ss, tok_rs, disp_ss, disp_rs, part_ss, part_rs, res_ss, res_rs, out_ss, out_rs,
 ):
     s = lax.axis_index("section")
@@ -206,6 +208,15 @@
         drain(meta_next, meta_rs.at[1])
         places(meta_next, place_next)
 
+        def join(m):
+            hop[m] = jnp.dot(place_next[m], chosen[m], preferred_element_type=jnp.float32).astype(jnp.bfloat16)
+            hop_scale[m] = jnp.dot(
+                place_next[m].astype(jnp.float32), scales[m],
+                preferred_element_type=jnp.float32, precision=lax.Precision.HIGHEST,
+            )
+
+        loop(PARTS, join)
+
     def spread(d):
         columns = pl.ds(pl.multiple_of(d * LANES, LANES), LANES)
         gains[d] = jnp.broadcast_to(gain_ref[0:1, columns], (SLOTS, LANES))
@@ -220,19 +231,21 @@
     def work(m, blocks):
         total = jnp.zeros((SLOTS, LANES), jnp.float32)
         acc = jnp.zeros((SLOTS, 2 * blocks * LANES), jnp.float32)
-        for r in NEAR_FIRST:
-            row = row_at(r)
-            four = pl.ds(row * GRID_X, GRID_X)
-            drain(disp_recv.at[m, four], disp_rs.at[m, r])
-            values = disp_recv[m, four].astype(jnp.float32)
-            gained = (values * gains[four]).astype(jnp.bfloat16)
-            for c in range(GRID_X):
-                total = total + values[c] * values[c]
-            acc = acc + jnp.dot(
-                jnp.concatenate([gained[c] for c in range(GRID_X)], axis=1),
-                wgu[row_columns(row), pl.ds(0, 2 * blocks * LANES)],
-                preferred_element_type=jnp.float32,
-            )
+        for group in ARRIVALS:
+            for r in group:
+                drain(disp_recv.at[m, pl.ds(row_at(r) * GRID_X, GRID_X)], disp_rs.at[m, r])
+            for r in group:
+                row = row_at(r)
+                four = pl.ds(row * GRID_X, GRID_X)
+                values = disp_recv[m, four].astype(jnp.float32)
+                gained = (values * gains[four]).astype(jnp.bfloat16)
+                for c in range(GRID_X):
+                    total = total + values[c] * values[c]
+                acc = acc + jnp.dot(
+                    jnp.concatenate([gained[c] for c in range(GRID_X)], axis=1),
+                    wgu[row_columns(row), pl.ds(0, 2 * blocks * LANES)],
+                    preferred_element_type=jnp.float32,
+                )
         inverse = lax.rsqrt(jnp.sum(total, axis=1, keepdims=True) * (1.0 / (PEERS * LANES)) + 1e-6)
         hidden = []
         for b in range(blocks):
@@ -240,38 +253,48 @@
             upward = acc[:, (2 * b + 1) * LANES:(2 * b + 2) * LANES] * inverse
             hidden.append((gate / (1.0 + jnp.exp(-gate)) * upward).astype(jnp.bfloat16))
         hidden = jnp.concatenate(hidden, axis=1)
-        for r in FAR_FIRST:
-            row = row_at(r)
-            part = jnp.dot(
-                hidden, wd[pl.ds(0, blocks * LANES), row_columns(row)], preferred_element_type=jnp.float32
-            ).astype(jnp.bfloat16)
-            for c in range(GRID_X):
-                part_send[m, row * GRID_X + c] = part[:, c * LANES:(c + 1) * LANES]
-            back = (GRID_Y - r) % GRID_Y
-            if blocks == 1:
-                in_row(
-                    r,
-                    lambda q, r: send(
-                        part_send.at[m, q], part_recv.at[m, p], part_ss, part_rs.at[m, r], s, q
-                    ),
-                    True,
-                )
-            else:
-                for j in range(2):
-                    send(
-                        part_send.at[m, pl.ds(row * GRID_X + 2 * j, PAIR)], part_recv.at[m, pl.ds(p, PAIR)],
-                        part_ss, part_rs.at[m, back], s, row * GRID_X + 2 * j + 1,
+        for group in LEAVING:
+            for r in group:
+                row = row_at(r)
+                part = jnp.dot(
+                    hidden, wd[pl.ds(0, blocks * LANES), row_columns(row)], preferred_element_type=jnp.float32
+                ).astype(jnp.bfloat16)
+                for c in range(GRID_X):
+                    part_send[m, row * GRID_X + c] = part[:, c * LANES:(c + 1) * LANES]
+            for r in group:
+                if blocks == 1:
+                    in_row(
+                        r,
+                        lambda q, r: send(
+                            part_send.at[m, q], part_recv.at[m, p], part_ss, part_rs.at[m, r], s, q
+                        ),
+                        True,
                     )
+                else:
+                    row = row_at(r)
+                    for j in range(2):
+                        send(
+                            part_send.at[m, pl.ds(row * GRID_X + 2 * j, PAIR)], part_recv.at[m, pl.ds(p, PAIR)],
+                            part_ss, part_rs.at[m, (GRID_Y - r) % GRID_Y], s, row * GRID_X + 2 * j + 1,
+                        )
         if blocks == 1:
             part_recv[m, p] = part_send[m, p]
 
     def keep(m):
-        for r in NEAR_FIRST:
-            row = row_at(r)
-            four = pl.ds(row * GRID_X, GRID_X)
-            drain(part_recv.at[m, four], part_rs.at[m, r])
-            values = part_recv[m, four].astype(jnp.float32)
-            pair_sums[row] = values[0:2] + values[2:4]
+        drain(res_recv.at[m], res_rs.at[m])
+
+        @pl.when(s < last)
+        def _():
+            for h in range(PAIR):
+                placed[h] = jnp.dot(place_next[m], res_recv[m, h], preferred_element_type=jnp.float32)
+
+        for group in ARRIVALS:
+            for r in group:
+                drain(part_recv.at[m, pl.ds(row_at(r) * GRID_X, GRID_X)], part_rs.at[m, r])
+            for r in group:
+                row = row_at(r)
+                values = part_recv[m, pl.ds(row * GRID_X, GRID_X)].astype(jnp.float32)
+                pair_sums[row] = values[0:2] + values[2:4]
         summed = []
         for h in range(PAIR):
             summed.append(
@@ -280,20 +303,16 @@
         summed = jnp.concatenate(summed, axis=1)
         high = summed.astype(jnp.bfloat16)
         low = (summed - high.astype(jnp.float32)).astype(jnp.bfloat16)
-        expert_out = jnp.dot(
-            chosen[m], jnp.concatenate([high, low], axis=0), preferred_element_type=jnp.float32
-        )
-        drain(res_recv.at[m], res_rs.at[m])
-        before = jnp.concatenate([res_recv[m, h] for h in range(PAIR)], axis=1).astype(jnp.float32)
-        scale = jnp.concatenate([scales[m]] * PAIR, axis=1)
-        rows = (before + scale * expert_out).astype(jnp.bfloat16)
+        both = jnp.concatenate([high, low], axis=0)
 
         @pl.when(s < last)
         def _():
-            slotted = jnp.dot(place_next[m], rows, preferred_element_type=jnp.float32).astype(jnp.bfloat16)
-            for e in range(EXPERTS):
-                for h in range(PAIR):
-                    pair_send[m, e, h] = slotted[e * SLOTS:(e + 1) * SLOTS, h * LANES:(h + 1) * LANES]
+            moved = jnp.dot(hop[m], both, preferred_element_type=jnp.float32)
+            for h in range(PAIR):
+                slotted = placed[h] + hop_scale[m] * moved[:, h * LANES:(h + 1) * LANES]
+                slotted = slotted.astype(jnp.bfloat16)
+                for e in range(EXPERTS):
+                    pair_send[m, e, h] = slotted[e * SLOTS:(e + 1) * SLOTS]
             for r in FAR_FIRST:
                 row = row_at(r)
                 for j in range(2):
@@ -301,6 +320,14 @@
                         pair_send.at[m, row // 2], disp_recv.at[m, pl.ds(p - 1, PAIR)],
                         disp_ss, disp_rs.at[m, (GRID_Y - r) % GRID_Y], s + 1, row * GRID_X + 2 * j,
                     )
+
+        expert_out = jnp.dot(chosen[m], both, preferred_element_type=jnp.float32)
+        before = jnp.concatenate([res_recv[m, h] for h in range(PAIR)], axis=1).astype(jnp.float32)
+        scale = jnp.concatenate([scales[m]] * PAIR, axis=1)
+        rows = (before + scale * expert_out).astype(jnp.bfloat16)
+
+        @pl.when(s < last)
+        def _():
             for h in range(PAIR):
                 pair_res[m, h] = rows[:, h * LANES:(h + 1) * LANES]
             send(pair_res.at[m], res_recv.at[m], res_ss, res_rs.at[m], s + 1, p)
@@ -468,6 +495,9 @@
             pltpu.VMEM((PARTS, EXPERTS, PAIR, SLOTS, LANES), b16),
             pltpu.VMEM((PARTS, PAIR, 64, LANES), b16),
             pltpu.VMEM((PARTS, 8, PAIR, 8, LANES), f32),
+            pltpu.VMEM((PARTS, 64, LANES), b16),
+            pltpu.VMEM((PARTS, 64, LANES), f32),
+            pltpu.VMEM((PAIR, 64, LANES), f32),
             dma((5,)),
             dma((3,)),
             dma((3,)),

time: 229 us -> 225 us (0.983)
  Pallas kernels: 227 us -> 224 us
    pallas_call x1, Pallas kernels: 227 us -> 224 us  [local(): pl.pallas_call(kernel, out_shape=jax.ShapeDtypeStruct((1, TOK, width), b1...]
where the time goes in v3:
time: 225 us
  Pallas kernels  224 us (100%)
    pallas_call x1, Pallas kernels, local(): pl.pallas_call(kernel, out_shape=jax.ShapeDtypeStruct((1, TOK, width), b1...  224 us

profile of v3, /device:TPU:505, one launch (start us, length us, event | category | flops | bytes accessed | tf_op | source)
XLA Modules:
  0.0 225.2 jit_solution(13747314339582431811)
XLA Ops:
  0.0 223.7 %shard_map.73 = bf16[1,6,4096]{2,1,0:T(8,128)(2,1)} custom-call(bf16[6,4096]{1,0:T(8,128)(2,1)} %tok_hbm.1, s32[1,6]{1,0:T(1,128)} %bitcast.1, f32[1,6]{1,0:T(1,128)} %scale_ref.1, f32[1,4096]{1,0:T(1,128)} %gain_hbm.1, bf16[1,4096,128]{2,1,0:T(8,128)(2,1)} %wg_hbm.1, bf16[1,4096,128]{2,1,0:T(8,128)(2,1)} %wu_hbm.1, bf16[1,128,4096]{2,1,0:T(8,128)(2,1)} %wd_hbm.1), custom_call_target="tpu_custom_call" | custom-call | tf_op jit(solution)/shard_map/pallas_call | solution.py:462
  223.7 1.5 copy.9

commit v4 on v3

--- a/solution.py
+++ b/solution.py
@@ -105,7 +105,10 @@
         meta_send[pl.ds(t, 1), :] = jnp.where(lane < 64, slot.astype(jnp.float32), scale_ref[0, t])
     lane = lax.broadcasted_iota(jnp.int32, (2, LANES), 1)
     meta_send[pl.ds(TOK, 2), :] = jnp.where(lane < 64, -1.0, 0.0)
-    meta_own[p] = meta_send[...]
+    @pl.when(s > 0)
+    def _():
+        meta_own[p] = meta_send[...]
+
 
     for load in near:
         load.wait()
@@ -145,6 +148,14 @@
                 (wd_hbm.at[0], wd.at[pl.ds(LANES, LANES)]),
             ))
         ]
+
+    @pl.when(s > 0)
+    def _():
+        everyone(lambda q, r: send(meta_send, meta_own.at[p], meta_ss, meta_rs.at[0], s, q), True)
+
+    @pl.when(late)
+    def _():
+        everyone(lambda q, r: send(meta_send, meta_next.at[p], meta_ss, meta_rs.at[1], s - 1, q), False)
 
     @pl.when(late & jnp.logical_not(worker))
     def _():
@@ -190,13 +201,15 @@
 
         lax.fori_loop(0, PARTS, first, 0)
 
-    everyone(lambda q, r: send(meta_send, meta_own.at[p], meta_ss, meta_rs.at[0], s, q), True)
+    pl.when(s == 1)(lambda: send(meta_init, meta_own, meta_ss, meta_rs.at[0], 0, p))
 
     @pl.when(s > 0)
     def _():
-        everyone(lambda q, r: send(meta_send, meta_next.at[p], meta_ss, meta_rs.at[1], s - 1, q), False)
-
-    drain(meta_own.at[pl.ds(0, PEERS - 1)], meta_rs.at[0])
+        drain(meta_own.at[pl.ds(0, PEERS - 1)], meta_rs.at[0])
+
+    pl.when(s == 1)(lambda: send(meta_own, meta_next, meta_ss, meta_rs.at[1], 0, p))
+
+    pl.when(s == 0)(lambda: drain(meta_own, meta_rs.at[0]))
     for m in range(PARTS):
         rows = meta_own[8 * m:8 * m + 8].reshape(64, LANES)
         lane = (lax.broadcasted_iota(jnp.int32, (64, LANES), 1) % 64).astype(jnp.float32)
@@ -416,9 +429,9 @@
 
     loop(PEERS, store)
 
-    drain(meta_own.at[pl.ds(0, PEERS - 1)], meta_ss)
-    pl.when(s > 0)(lambda: drain(meta_own, meta_ss))
-    pl.when(s == 0)(lambda: drain(meta_own, meta_ss))
+    drain(meta_own, meta_ss)
+    pl.when(s > 0)(lambda: drain(meta_own.at[pl.ds(0, PEERS - 1)], meta_ss))
+    pl.when(s == 1)(lambda: drain(meta_own, meta_ss))
 
     half = PEERS // 2
 

time: 225 us -> 217 us (0.964)
  Pallas kernels: 224 us -> 215 us
    pallas_call x1, Pallas kernels: 224 us -> 215 us  [local(): pl.pallas_call(kernel, out_shape=jax.ShapeDtypeStruct((1, TOK, width), b1...]
where the time goes in v4:
time: 217 us; the launch traced here: 216 us
  Pallas kernels  215 us (99%)
    pallas_call x1, Pallas kernels, local(): pl.pallas_call(kernel, out_shape=jax.ShapeDtypeStruct((1, TOK, width), b1...  215 us

profile of v4, /device:TPU:505, one launch (start us, length us, event | category | flops | bytes accessed | tf_op | source)
XLA Modules:
  0.0 216.4 jit_solution(6241020650936691393)
XLA Ops:
  0.0 214.9 %shard_map.73 = bf16[1,6,4096]{2,1,0:T(8,128)(2,1)} custom-call(bf16[6,4096]{1,0:T(8,128)(2,1)} %tok_hbm.1, s32[1,6]{1,0:T(1,128)} %bitcast.1, f32[1,6]{1,0:T(1,128)} %scale_ref.1, f32[1,4096]{1,0:T(1,128)} %gain_hbm.1, bf16[1,4096,128]{2,1,0:T(8,128)(2,1)} %wg_hbm.1, bf16[1,4096,128]{2,1,0:T(8,128)(2,1)} %wu_hbm.1, bf16[1,128,4096]{2,1,0:T(8,128)(2,1)} %wd_hbm.1), custom_call_target="tpu_custom_call" | custom-call | tf_op jit(solution)/shard_map/pallas_call | solution.py:475
  214.9 1.5 copy.9

commit v5 on v4

--- a/solution.py
+++ b/solution.py
@@ -301,7 +301,7 @@
             for h in range(PAIR):
                 placed[h] = jnp.dot(place_next[m], res_recv[m, h], preferred_element_type=jnp.float32)
 
-        for group in ARRIVALS:
+        for group in (NEAR_FIRST,):
             for r in group:
                 drain(part_recv.at[m, pl.ds(row_at(r) * GRID_X, GRID_X)], part_rs.at[m, r])
             for r in group:

time: 217 us -> 216 us (level)
  no operation moved by 1% of the time
where the time goes in v5:
time: 216 us
  Pallas kernels  215 us (100%)
    pallas_call x1, Pallas kernels, local(): pl.pallas_call(kernel, out_shape=jax.ShapeDtypeStruct((1, TOK, width), b1...  215 us

profile of v5, /device:TPU:505, one launch (start us, length us, event | category | flops | bytes accessed | tf_op | source)
XLA Modules:
  0.0 216.0 jit_solution(9951760105148999928)
XLA Ops:
  0.0 214.5 %shard_map.73 = bf16[1,6,4096]{2,1,0:T(8,128)(2,1)} custom-call(bf16[6,4096]{1,0:T(8,128)(2,1)} %tok_hbm.1, s32[1,6]{1,0:T(1,128)} %bitcast.1, f32[1,6]{1,0:T(1,128)} %scale_ref.1, f32[1,4096]{1,0:T(1,128)} %gain_hbm.1, bf16[1,4096,128]{2,1,0:T(8,128)(2,1)} %wg_hbm.1, bf16[1,4096,128]{2,1,0:T(8,128)(2,1)} %wu_hbm.1, bf16[1,128,4096]{2,1,0:T(8,128)(2,1)} %wd_hbm.1), custom_call_target="tpu_custom_call" | custom-call | tf_op jit(solution)/shard_map/pallas_call | solution.py:475
  214.5 1.5 copy.9
